TPU v7x, 128 devices: a whole 4x4x4 slice. The times are simulated.
128 devices in a mesh: dp: 16 (over z, y), row: 2 (over x_lo), col: 4 (over x_hi, core).
Axes of the slice: x: 4 (x_hi: 2, x_lo: 2; x = x_hi * 2 + x_lo), y: 4, z: 4, core: 2. Of those that a mesh axis runs over, the one named last changes fastest.
Arguments:
- hidden_in: bfloat16 [8192, 1024], P(('dp', 'row'), 'col'), may hold values from -6 to 6
- seg_ids: int32 [8192], P(('dp', 'row')), may hold values from 0 to 7, as said below
- key_mask: int32 [8192], P(('dp', 'row')), may hold values 0 or 1
- w_qkv: bfloat16 [2, 1024, 3, 1024], P(None, 'row', None, 'col'), may hold values from -0.1875 to 0.1875
- qv_bias: float32 [2, 2, 1024], P(None, None, 'col'), may hold values from -4 to 4
- w_out: bfloat16 [2, 1024, 1024], P(None, 'col', 'row'), may hold values from -2 to 2
- out_bias: float32 [2, 1024], P(None, 'col'), may hold values from -4 to 4
- ln_gain: float32 [2, 2, 1024], P(None, None, 'col'), may hold values from 0.5 to 1.5
- ln_shift: float32 [2, 2, 1024], P(None, None, 'col'), may hold values from -4 to 4
- w_up: bfloat16 [2, 1024, 4096], P(None, 'row', 'col'), may hold values from -0.1875 to 0.1875
- up_bias: float32 [2, 4096], P(None, 'col'), may hold values from -6 to 6
- w_down: bfloat16 [2, 4096, 1024], P(None, 'col', 'row'), may hold values from -0.09375 to 0.09375
- down_bias: float32 [2, 1024], P(None, 'col'), may hold values from -4 to 4
- grad_out: bfloat16 [8192, 1024], P(('dp', 'row'), 'col'), may hold values from -6 to 6
Outputs:
- hidden_out: bfloat16 [8192, 1024], P(('dp', 'row'), 'col')
- grad_in: bfloat16 [8192, 1024], P(('dp', 'row'), 'col')
- grad_w_qkv: float32 [2, 1024, 3, 1024], P(None, 'row', None, 'col')
- grad_qv_bias: float32 [2, 2, 1024], P(None, None, 'col')
- grad_w_out: float32 [2, 1024, 1024], P(None, 'col', 'row')
- grad_out_bias: float32 [2, 1024], P(None, 'col')
- grad_ln_gain: float32 [2, 2, 1024], P(None, None, 'col')
- grad_ln_shift: float32 [2, 2, 1024], P(None, None, 'col')
- grad_w_up: float32 [2, 1024, 4096], P(None, 'row', 'col')
- grad_up_bias: float32 [2, 4096], P(None, 'col')
- grad_w_down: float32 [2, 4096, 1024], P(None, 'col', 'row')
- grad_down_bias: float32 [2, 1024], P(None, 'col')
Inputs may be any that keep to these rules, and one draw needn't show every extreme that they name: `seg_ids`: within each aligned block of 256 tokens the ids start at 0 and never fall; a change of id starts a new sequence. In every draw one block holds a single sequence of 256 tokens, and some block reaches the largest id.
All inputs are finite; a program needn't handle non-finite values. No bound on the sum of `key_mask` on one device may be relied on, other than what follows from the above.
Results may differ from a plain program's by a relative error of at most 0.035.
Values may be sent and summed in bfloat16 or wider, within the bound.
A program may use at most 128 MiB of HBM per device.

v0:
```python
import jax
import jax.numpy as jnp
from jax import lax
from jax.sharding import PartitionSpec as P

D = 1024
HD = 64
LAYERS = 2


EPSILON = 1e-05
MASKED = -1e30


def gather_features(values_in):
    return lax.all_gather(values_in, "col", axis=1, tiled=True)


def gather_rows(weight):
    return lax.all_gather(weight, "row", axis=0, tiled=True)


def gather_cols(weight):
    return lax.all_gather(weight, "row", axis=1, tiled=True)


def sum_parts(values_in):
    return lax.psum_scatter(
        values_in.astype(jnp.bfloat16), "col", scatter_dimension=1, tiled=True
    ).astype(jnp.float32)


def sum_data(partial_value):
    return lax.psum(partial_value.astype(jnp.bfloat16), "dp").astype(jnp.float32)


def reduce_rows(gradient):
    return sum_data(
        lax.psum_scatter(
            gradient.astype(jnp.bfloat16), "row", scatter_dimension=0, tiled=True
        ).astype(jnp.float32)
    )


def reduce_cols(gradient):
    return sum_data(
        lax.psum_scatter(
            gradient.astype(jnp.bfloat16), "row", scatter_dimension=1, tiled=True
        ).astype(jnp.float32)
    )


def norm_forward(values_in, gain_vec, shift_vec):
    row_total, squares = lax.psum(
        (jnp.sum(values_in, axis=1), jnp.sum(values_in * values_in, axis=1)), "col"
    )
    mean_row = row_total / D
    inverse = lax.rsqrt(squares / D - mean_row * mean_row + EPSILON)
    normed = (values_in - mean_row[:, None]) * inverse[:, None]
    return (normed * gain_vec + shift_vec, normed, inverse)


def norm_backward(upstream, normed, inverse, gain_vec):
    scaled_grad = upstream * gain_vec
    row_total, along = lax.psum(
        (jnp.sum(scaled_grad, axis=1), jnp.sum(scaled_grad * normed, axis=1)), "col"
    )
    return inverse[:, None] * (scaled_grad - row_total[:, None] / D - normed * (along[:, None] / D))


def block_scores(row_start, block_rows, queries, keyset, seg_ids, key_mask):
    tok_rows = seg_ids.shape[0]
    query_place = row_start + jnp.arange(block_rows, dtype=jnp.int32)
    key_place = jnp.arange(tok_rows, dtype=jnp.int32)
    allowed = (seg_ids[:, None] == seg_ids[None, :]) & (
        (key_mask[None, :] == 1) | (query_place[:, None] == key_place[None, :])
    )
    scores = jnp.einsum("qhd,khd->hqk", queries, keyset, preferred_element_type=jnp.float32)
    scaled = jnp.where(allowed[None], scores * HD ** (-0.5), MASKED)
    return (queries, scaled, allowed)


def attend_forward(queries, keyset, valueset, seg_ids, key_mask, block_rows):
    tok_rows, head_count, head_size = queries.shape

    def one_block(row_start):
        query_block, scaled, allowed = block_scores(
            row_start, block_rows, queries, keyset, seg_ids, key_mask
        )
        highest = jnp.max(scaled, axis=2, keepdims=True)
        raised = jnp.exp(scaled - highest)
        row_total = jnp.sum(raised, axis=2, keepdims=True)
        probs_low = (raised / row_total).astype(jnp.bfloat16)
        context = jnp.einsum(
            "hqk,khd->qhd", probs_low, valueset, preferred_element_type=jnp.float32
        )
        return (context.astype(jnp.bfloat16), (highest + jnp.log(row_total))[:, :, 0])

    starts = jnp.arange(tok_rows // block_rows, dtype=jnp.int32) * block_rows
    context, log_totals = lax.map(one_block, starts)
    return (context.reshape(tok_rows, head_count * head_size), log_totals)


def attend_backward(
    queries, keyset, valueset, grad_context, log_totals, seg_ids, key_mask, block_rows
):
    tok_rows, head_count, head_size = queries.shape
    grad_heads = grad_context.reshape(tok_rows, head_count, head_size)

    def one_block(carry, members):
        row_start, log_block = members
        grad_keys, grad_values = carry
        query_block, scaled, allowed = block_scores(
            row_start, block_rows, queries, keyset, seg_ids, key_mask
        )
        probs = jnp.where(allowed[None], jnp.exp(scaled - log_block[:, :, None]), 0.0)
        grad_probs = jnp.einsum(
            "qhd,khd->hqk", grad_heads, valueset, preferred_element_type=jnp.float32
        )
        centre = jnp.sum(probs * grad_probs, axis=2, keepdims=True)
        grad_scores = (probs * (grad_probs - centre) * HD ** (-0.5)).astype(jnp.bfloat16)
        grad_query = jnp.einsum(
            "hqk,khd->qhd", grad_scores, keyset, preferred_element_type=jnp.float32
        )
        grad_keys = grad_keys + jnp.einsum(
            "hqk,qhd->khd", grad_scores, query_block, preferred_element_type=jnp.float32
        )
        grad_values = grad_values + jnp.einsum(
            "hqk,qhd->khd",
            probs.astype(jnp.bfloat16),
            grad_heads,
            preferred_element_type=jnp.float32,
        )
        return ((grad_keys, grad_values), grad_query)

    starts = jnp.arange(tok_rows // block_rows, dtype=jnp.int32) * block_rows
    zeros_init = jnp.zeros((tok_rows, head_count, head_size), jnp.float32)
    (grad_keys, grad_values), grad_query = lax.scan(
        one_block, (zeros_init, zeros_init), (starts, log_totals)
    )
    width_local = head_count * head_size
    return (
        grad_query.reshape(tok_rows, width_local),
        grad_keys.reshape(tok_rows, width_local),
        grad_values.reshape(tok_rows, width_local),
    )


def shards(
    hidden_in,
    seg_ids,
    key_mask,
    w_qkv,
    qv_bias,
    w_out,
    out_bias,
    ln_gain,
    ln_shift,
    w_up,
    up_bias,
    w_down,
    down_bias,
    grad_out,
):
    tok_rows = hidden_in.shape[0]
    block_rows = min(512, tok_rows)
    head_count = w_qkv.shape[3] // HD
    stream = hidden_in.astype(jnp.float32)
    saved_layers = []
    for layer_index in range(LAYERS):
        state_full = gather_features(stream.astype(jnp.bfloat16))
        qkv_full = gather_rows(w_qkv[layer_index])
        mixed_all = jnp.einsum(
            "td,dje->tje", state_full, qkv_full, preferred_element_type=jnp.float32
        )
        queries = (
            (mixed_all[:, 0] + qv_bias[layer_index, 0])
            .astype(jnp.bfloat16)
            .reshape(tok_rows, head_count, HD)
        )
        keyset = mixed_all[:, 1].astype(jnp.bfloat16).reshape(tok_rows, head_count, HD)
        valueset = (
            (mixed_all[:, 2] + qv_bias[layer_index, 1])
            .astype(jnp.bfloat16)
            .reshape(tok_rows, head_count, HD)
        )
        context, log_totals = attend_forward(
            queries, keyset, valueset, seg_ids, key_mask, block_rows
        )
        out_full = gather_cols(w_out[layer_index])
        first = (
            stream
            + sum_parts(jnp.dot(context, out_full, preferred_element_type=jnp.float32))
            + out_bias[layer_index]
        )
        middle, normed_one, inverse_one = norm_forward(
            first, ln_gain[layer_index, 0], ln_shift[layer_index, 0]
        )
        middle_full = gather_features(middle.astype(jnp.bfloat16))
        up_full = gather_rows(w_up[layer_index])
        lifted = (
            jnp.dot(middle_full, up_full, preferred_element_type=jnp.float32) + up_bias[layer_index]
        )
        activated = jax.nn.gelu(lifted, approximate=False).astype(jnp.bfloat16)
        down_full = gather_cols(w_down[layer_index])
        second = (
            middle
            + sum_parts(jnp.dot(activated, down_full, preferred_element_type=jnp.float32))
            + down_bias[layer_index]
        )
        stream, normed_two, inverse_two = norm_forward(
            second, ln_gain[layer_index, 1], ln_shift[layer_index, 1]
        )
        saved_layers.append(
            (
                state_full,
                queries,
                keyset,
                valueset,
                context,
                log_totals,
                normed_one,
                inverse_one,
                middle_full,
                lifted,
                activated,
                normed_two,
                inverse_two,
                (qkv_full, out_full, up_full, down_full),
            )
        )
    qkv_grads = [None] * LAYERS
    qv_grads = [None] * LAYERS
    out_grads = [None] * LAYERS
    outb_grads = [None] * LAYERS
    gain_grads = [None] * LAYERS
    shift_grads = [None] * LAYERS
    up_grads = [None] * LAYERS
    upb_grads = [None] * LAYERS
    down_grads = [None] * LAYERS
    downb_grads = [None] * LAYERS
    upstream = grad_out.astype(jnp.float32)
    for layer_index in reversed(range(LAYERS)):
        (
            state_full,
            queries,
            keyset,
            valueset,
            context,
            log_totals,
            normed_one,
            inverse_one,
            middle_full,
            lifted,
            activated,
            normed_two,
            inverse_two,
            gathered,
        ) = saved_layers[layer_index]
        qkv_full = gather_rows(w_qkv[layer_index])
        out_full = gather_cols(w_out[layer_index])
        up_full = gather_rows(w_up[layer_index])
        down_full = gather_cols(w_down[layer_index])
        gain_two = jnp.sum(upstream * normed_two, axis=0)
        shift_two = jnp.sum(upstream, axis=0)
        grad_second = norm_backward(upstream, normed_two, inverse_two, ln_gain[layer_index, 1])
        downb_grads[layer_index] = jnp.sum(grad_second, axis=0)
        second_full = gather_features(grad_second.astype(jnp.bfloat16))
        down_grads[layer_index] = reduce_cols(
            jnp.einsum("tf,td->fd", activated, second_full, preferred_element_type=jnp.float32)
        )
        grad_act = jnp.einsum(
            "td,fd->tf", second_full, down_full, preferred_element_type=jnp.float32
        )
        gelu_value, gelu_pull = jax.vjp(lambda inner: jax.nn.gelu(inner, approximate=False), lifted)
        grad_lifted = gelu_pull(grad_act)[0]
        upb_grads[layer_index] = jnp.sum(grad_lifted, axis=0)
        lifted_low = grad_lifted.astype(jnp.bfloat16)
        up_grads[layer_index] = reduce_rows(
            jnp.einsum("td,tf->df", middle_full, lifted_low, preferred_element_type=jnp.float32)
        )
        grad_middle = grad_second + sum_parts(
            jnp.einsum("tf,df->td", lifted_low, up_full, preferred_element_type=jnp.float32)
        )
        gain_one = jnp.sum(grad_middle * normed_one, axis=0)
        shift_one = jnp.sum(grad_middle, axis=0)
        gain_grads[layer_index] = jnp.stack([gain_one, gain_two])
        shift_grads[layer_index] = jnp.stack([shift_one, shift_two])
        grad_first = norm_backward(grad_middle, normed_one, inverse_one, ln_gain[layer_index, 0])
        outb_grads[layer_index] = jnp.sum(grad_first, axis=0)
        first_full = gather_features(grad_first.astype(jnp.bfloat16))
        out_grads[layer_index] = reduce_cols(
            jnp.einsum("te,td->ed", context, first_full, preferred_element_type=jnp.float32)
        )
        grad_context = jnp.einsum(
            "td,ed->te", first_full, out_full, preferred_element_type=jnp.float32
        ).astype(jnp.bfloat16)
        grad_query, grad_key, grad_value = attend_backward(
            queries, keyset, valueset, grad_context, log_totals, seg_ids, key_mask, block_rows
        )
        qv_grads[layer_index] = jnp.stack(
            [jnp.sum(grad_query, axis=0), jnp.sum(grad_value, axis=0)]
        )
        mixed_low = jnp.stack([grad_query, grad_key, grad_value], axis=1).astype(jnp.bfloat16)
        qkv_grads[layer_index] = reduce_rows(
            jnp.einsum("td,tje->dje", state_full, mixed_low, preferred_element_type=jnp.float32)
        )
        upstream = grad_first + sum_parts(
            jnp.einsum("tje,dje->td", mixed_low, qkv_full, preferred_element_type=jnp.float32)
        )
    small_sums = lax.psum(
        (
            jnp.stack(qv_grads),
            jnp.stack(outb_grads),
            jnp.stack(gain_grads),
            jnp.stack(shift_grads),
            jnp.stack(upb_grads),
            jnp.stack(downb_grads),
        ),
        ("dp", "row"),
    )
    return (
        stream.astype(jnp.bfloat16),
        upstream.astype(jnp.bfloat16),
        jnp.stack(qkv_grads),
        small_sums[0],
        jnp.stack(out_grads),
        small_sums[1],
        small_sums[2],
        small_sums[3],
        jnp.stack(up_grads),
        small_sums[4],
        jnp.stack(down_grads),
        small_sums[5],
    )


def solution(mesh):
    return jax.shard_map(
        shards,
        mesh=mesh,
        in_specs=(
            P(("dp", "row"), "col"),
            P(("dp", "row")),
            P(("dp", "row")),
            P(None, "row", None, "col"),
            P(None, None, "col"),
            P(None, "col", "row"),
            P(None, "col"),
            P(None, None, "col"),
            P(None, None, "col"),
            P(None, "row", "col"),
            P(None, "col"),
            P(None, "col", "row"),
            P(None, "col"),
            P(("dp", "row"), "col"),
        ),
        out_specs=(
            P(("dp", "row"), "col"),
            P(("dp", "row"), "col"),
            P(None, "row", None, "col"),
            P(None, None, "col"),
            P(None, "col", "row"),
            P(None, "col"),
            P(None, None, "col"),
            P(None, None, "col"),
            P(None, "row", "col"),
            P(None, "col"),
            P(None, "col", "row"),
            P(None, "col"),
        ),
        check_vma=False,
    )
```

profile of v0, /device:TPU:0, one launch (start us, length us, event | category | flops | bytes accessed | tf_op | source)
XLA Modules:
  0.0 983.7 jit_solution(16687585207563004637)
XLA Ops:
  28.0 15.4 %all-gather.15.cloned.1.call-done = bf16[1,1024,3,256]{1,3,2,0:T(8,128)(2,1)} async-done(((bf16[1,512,3,256]{1,3,2,0:T(8,128)(2,1)}), bf16[1,1024,3,256]{1,3,2,0:T(8,128)(2,1)}) %all-gather.15.cloned.1.call-update) | async-done | bytes 1572880 | tf_op jit(solution)/shard_map/all_gather | solution.py:20
  56.3 22.4 %reduce-scatter.17.cloned.1.call-done = bf16[256,256]{1,0:T(8,128)(2,1)} async-done(((bf16[256,1024]{1,0:T(8,128)(2,1)}), bf16[256,256]{1,0:T(8,128)(2,1)}) %reduce-scatter.17.cloned.1.call-update) | async-done | bytes 131088 | tf_op jit(solution)/shard_map/reduce_scatter | solution.py:28
  88.1 10.5 %all_gather.59 = bf16[256,1024]{1,0:T(8,128)(2,1)S(1)} all-gather(bf16[256,256]{1,0:T(8,128)(2,1)S(1)} %fusion.120), channel_id=1, replica_groups=mesh['dp'=16,'row'=2,'col'=4] {'col'}, dimensions={1}, use_global_device_ids=true | all-gather | bytes 655360 | tf_op jit(solution)/shard_map/all_gather | solution.py:16
  98.6 18.9 %all-gather.17.cloned.1.call-done = bf16[1,1024,1024]{2,1,0:T(8,128)(2,1)} async-done(((bf16[1,512,1024]{2,1,0:T(8,128)(2,1)}), bf16[1,1024,1024]{2,1,0:T(8,128)(2,1)}) %all-gather.17.cloned.1.call-update) | async-done | bytes 2097168 | tf_op jit(solution)/shard_map/all_gather | solution.py:20
  123.0 32.8 %all-gather.19.cloned.1.call-done = bf16[1,1024,1024]{2,1,0:T(8,128)(2,1)} async-done(((bf16[1,1024,512]{2,1,0:T(8,128)(2,1)}), bf16[1,1024,1024]{2,1,0:T(8,128)(2,1)}) %all-gather.19.cloned.1.call-update) | async-done | bytes 2097168 | tf_op jit(solution)/shard_map/all_gather | solution.py:24
  169.7 18.9 %reduce-scatter.19.cloned.1.call-done = bf16[256,256]{1,0:T(8,128)(2,1)} async-done(((bf16[256,1024]{1,0:T(8,128)(2,1)}), bf16[256,256]{1,0:T(8,128)(2,1)}) %reduce-scatter.19.cloned.1.call-update) | async-done | bytes 131088 | tf_op jit(solution)/shard_map/reduce_scatter | solution.py:28
  197.2 10.9 %all_gather.62 = bf16[256,1024]{1,0:T(8,128)(2,1)S(1)} all-gather(bf16[256,256]{1,0:T(8,128)(2,1)S(1)} %fusion.121), channel_id=1, replica_groups=mesh['dp'=16,'row'=2,'col'=4] {'col'}, dimensions={1}, use_global_device_ids=true | all-gather | bytes 655360 | tf_op jit(solution)/shard_map/all_gather | solution.py:16
  208.1 12.7 %all-gather.21.cloned.1.call-done = bf16[1,1024,3,256]{1,3,2,0:T(8,128)(2,1)} async-done(((bf16[1,512,3,256]{1,3,2,0:T(8,128)(2,1)}), bf16[1,1024,3,256]{1,3,2,0:T(8,128)(2,1)}) %all-gather.21.cloned.1.call-update) | async-done | bytes 1572880 | tf_op jit(solution)/shard_map/all_gather | solution.py:20
  227.4 28.1 %reduce-scatter.21.cloned.1.call-done = bf16[256,256]{1,0:T(8,128)(2,1)} async-done(((bf16[256,1024]{1,0:T(8,128)(2,1)}), bf16[256,256]{1,0:T(8,128)(2,1)}) %reduce-scatter.21.cloned.1.call-update) | async-done | bytes 131088 | tf_op jit(solution)/shard_map/reduce_scatter | solution.py:28
  264.1 9.9 %all_gather.65 = bf16[256,1024]{1,0:T(8,128)(2,1)S(1)} all-gather(bf16[256,256]{1,0:T(8,128)(2,1)S(1)} %fusion.122), channel_id=1, replica_groups=mesh['dp'=16,'row'=2,'col'=4] {'col'}, dimensions={1}, use_global_device_ids=true | all-gather | bytes 655360 | tf_op jit(solution)/shard_map/all_gather | solution.py:16
  274.0 20.3 %all-gather.23.cloned.1.call-done = bf16[1,1024,1024]{2,1,0:T(8,128)(2,1)} async-done(((bf16[1,512,1024]{2,1,0:T(8,128)(2,1)}), bf16[1,1024,1024]{2,1,0:T(8,128)(2,1)}) %all-gather.23.cloned.1.call-update) | async-done | bytes 2097168 | tf_op jit(solution)/shard_map/all_gather | solution.py:20
  299.8 32.9 %all-gather.25.cloned.1.call-done = bf16[1,1024,1024]{2,1,0:T(8,128)(2,1)} async-done(((bf16[1,1024,512]{2,1,0:T(8,128)(2,1)}), bf16[1,1024,1024]{2,1,0:T(8,128)(2,1)}) %all-gather.25.cloned.1.call-update) | async-done | bytes 2097168 | tf_op jit(solution)/shard_map/all_gather | solution.py:24
  336.1 29.6 %reduce-scatter.23.cloned.1.call-done = bf16[256,256]{1,0:T(8,128)(2,1)} async-done(((bf16[256,1024]{1,0:T(8,128)(2,1)}), bf16[256,256]{1,0:T(8,128)(2,1)}) %reduce-scatter.23.cloned.1.call-update) | async-done | bytes 131088 | tf_op jit(solution)/shard_map/reduce_scatter | solution.py:28
  399.0 29.5 %reduce-scatter.25.cloned.1.call-done = bf16[256,256]{1,0:T(8,128)(2,1)} async-done(((bf16[256,1024]{1,0:T(8,128)(2,1)}), bf16[256,256]{1,0:T(8,128)(2,1)}) %reduce-scatter.25.cloned.1.call-update) | async-done | bytes 131088 | tf_op jit(solution)/shard_map/reduce_scatter | solution.py:28
  461.0 29.3 %reduce-scatter.27.cloned.1.call-done = bf16[256,256]{1,0:T(8,128)(2,1)} async-done(((bf16[256,1024]{1,0:T(8,128)(2,1)}), bf16[256,256]{1,0:T(8,128)(2,1)}) %reduce-scatter.27.cloned.1.call-update) | async-done | bytes 131088 | tf_op jit(solution)/shard_map/reduce_scatter | solution.py:28
  516.9 28.1 %reduce-scatter.29.cloned.1.call-done = bf16[256,256]{1,0:T(8,128)(2,1)} async-done(((bf16[256,1024]{1,0:T(8,128)(2,1)}), bf16[256,256]{1,0:T(8,128)(2,1)}) %reduce-scatter.29.cloned.1.call-update) | async-done | bytes 131088 | tf_op jit(solution)/shard_map/reduce_scatter | solution.py:28
  556.0 11.9 %all_gather.71 = bf16[256,1024]{1,0:T(8,128)(2,1)S(1)} all-gather(bf16[256,256]{1,0:T(8,128)(2,1)S(1)} %convert_element_type.259), channel_id=1, replica_groups=mesh['dp'=16,'row'=2,'col'=4] {'col'}, dimensions={1}, use_global_device_ids=true | all-gather | bytes 655360 | tf_op jit(solution)/shard_map/all_gather | solution.py:16
  595.6 23.1 %reduce-scatter.35.cloned.1.call-done = bf16[512,3,256]{0,2,1:T(8,128)(2,1)} async-done(((bf16[1024,3,256]{0,2,1:T(8,128)(2,1)}), bf16[512,3,256]{0,2,1:T(8,128)(2,1)}) %reduce-scatter.35.cloned.1.call-update) | async-done | bytes 786448 | tf_op jit(solution)/shard_map/reduce_scatter | solution.py:39
  618.7 38.1 %reduce-scatter.47.cloned.1.call-done = bf16[1024,512]{1,0:T(8,128)(2,1)} async-done(((bf16[1024,1024]{1,0:T(8,128)(2,1)}), bf16[1024,512]{1,0:T(8,128)(2,1)}) %reduce-scatter.47.cloned.1.call-update) | async-done | bytes 1048592 | tf_op jit(solution)/shard_map/reduce_scatter | solution.py:47
  656.8 38.2 %reduce-scatter.43.cloned.1.call-done = bf16[512,1024]{1,0:T(8,128)(2,1)} async-done(((bf16[1024,1024]{1,0:T(8,128)(2,1)}), bf16[512,1024]{1,0:T(8,128)(2,1)}) %reduce-scatter.43.cloned.1.call-update) | async-done | bytes 1048592 | tf_op jit(solution)/shard_map/reduce_scatter | solution.py:39
  695.1 31.9 %reduce-scatter.33.cloned.1.call-done = bf16[512,3,256]{0,2,1:T(8,128)(2,1)} async-done(((bf16[1024,3,256]{0,2,1:T(8,128)(2,1)}), bf16[512,3,256]{0,2,1:T(8,128)(2,1)}) %reduce-scatter.33.cloned.1.call-update) | async-done | bytes 786448 | tf_op jit(solution)/shard_map/reduce_scatter | solution.py:39
  727.0 37.7 %reduce-scatter.45.cloned.1.call-done = bf16[1024,512]{1,0:T(8,128)(2,1)} async-done(((bf16[1024,1024]{1,0:T(8,128)(2,1)}), bf16[1024,512]{1,0:T(8,128)(2,1)}) %reduce-scatter.45.cloned.1.call-update) | async-done | bytes 1048592 | tf_op jit(solution)/shard_map/reduce_scatter | solution.py:47
  764.7 38.3 %reduce-scatter.41.cloned.1.call-done = bf16[512,1024]{1,0:T(8,128)(2,1)} async-done(((bf16[1024,1024]{1,0:T(8,128)(2,1)}), bf16[512,1024]{1,0:T(8,128)(2,1)}) %reduce-scatter.41.cloned.1.call-update) | async-done | bytes 1048592 | tf_op jit(solution)/shard_map/reduce_scatter | solution.py:39
  804.3 159.4 %all-reduce = (f32[2,2,256]{2,1,0:T(2,128)}, f32[2,256]{1,0:T(2,128)}, f32[2,2,256]{2,1,0:T(2,128)}, f32[2,2,256]{2,1,0:T(2,128)}, f32[2,1024]{1,0:T(2,128)}, /*index=5*/f32[2,256]{1,0:T(2,128)}) all-reduce(f32[2,2,256]{2,1,0:T(2,128)S(1)} %pad_maximum_fusion.7, ...), channel_id=1, replica_groups=mesh['dp'=16,'row'=2,'col'=4] {'dp','row'}, use_global_device_ids=true, to_apply=%region_54.55 | all-reduce | flops 6144 | bytes 49152 | tf_op jit(solution)/shard_map/psum | solution.py:311
  (335 shorter events, 239.5 us)
Async XLA Ops:
  7.2 36.2 %all-gather.15.cloned.1.call-start = ((), (), s32[]{:S(2)}) async-start(), calls=%async_computation.32 | async-start | bytes 2359296 | tf_op jit(solution)/shard_map/all_gather | solution.py:20
  10.0 68.7 %reduce-scatter.17.cloned.1.call-start = ((), (), s32[]{:S(2)}) async-start(), calls=%async_computation.16 | async-start | bytes 655360 | tf_op jit(solution)/shard_map/reduce_scatter | solution.py:28
  48.8 68.8 %all-gather.17.cloned.1.call-start = ((), (), s32[]{:S(2)}) async-start(), calls=%async_computation.33 | async-start | bytes 3145728 | tf_op jit(solution)/shard_map/all_gather | solution.py:20
  51.9 103.9 %all-gather.19.cloned.1.call-start = ((), (), s32[]{:S(2)}) async-start(), calls=%async_computation.34 | async-start | bytes 3145728 | tf_op jit(solution)/shard_map/all_gather | solution.py:24
  55.0 133.6 %reduce-scatter.19.cloned.1.call-start = ((), (), s32[]{:S(2)}) async-start(), calls=%async_computation.17 | async-start | bytes 655360 | tf_op jit(solution)/shard_map/reduce_scatter | solution.py:28
  158.9 61.8 %all-gather.21.cloned.1.call-start = ((), (), s32[]{:S(2)}) async-start(), calls=%async_computation.35 | async-start | bytes 2359296 | tf_op jit(solution)/shard_map/all_gather | solution.py:20
  160.2 95.3 %reduce-scatter.21.cloned.1.call-start = ((), (), s32[]{:S(2)}) async-start(), calls=%async_computation.18 | async-start | bytes 655360 | tf_op jit(solution)/shard_map/reduce_scatter | solution.py:28
  225.8 68.5 %copy-start.65 = (f32[1,1024]{1,0:T(1,128)S(1)}, f32[1,1024]{1,0:T(1,128)}, u32[]{:S(2)}) copy-start(f32[1,1024]{1,0:T(1,128)} %get-tuple-element.235) | copy-start | bytes 12292
  225.8 68.5 %all-gather.23.cloned.1.call-start = ((), (), s32[]{:S(2)}) async-start(), calls=%async_computation.36 | async-start | bytes 3145728 | tf_op jit(solution)/shard_map/all_gather | solution.py:20
  226.6 106.1 %all-gather.25.cloned.1.call-start = ((), (), s32[]{:S(2)}) async-start(), calls=%async_computation.37 | async-start | bytes 3145728 | tf_op jit(solution)/shard_map/all_gather | solution.py:24
  227.3 138.4 %reduce-scatter.23.cloned.1.call-start = ((), (), s32[]{:S(2)}) async-start(), calls=%async_computation.19 | async-start | bytes 655360 | tf_op jit(solution)/shard_map/reduce_scatter | solution.py:28
  336.0 92.5 %reduce-scatter.25.cloned.1.call-start = ((), (), s32[]{:S(2)}) async-start(), calls=%async_computation.20 | async-start | bytes 655360 | tf_op jit(solution)/shard_map/reduce_scatter | solution.py:28
  399.0 91.4 %reduce-scatter.27.cloned.1.call-start = ((), (), s32[]{:S(2)}) async-start(), calls=%async_computation.21 | async-start | bytes 655360 | tf_op jit(solution)/shard_map/reduce_scatter | solution.py:28
  461.0 84.1 %reduce-scatter.29.cloned.1.call-start = ((), (), s32[]{:S(2)}) async-start(), calls=%async_computation.22 | async-start | bytes 655360 | tf_op jit(solution)/shard_map/reduce_scatter | solution.py:28
  515.7 79.9 %reduce-scatter.39.cloned.1.call-start = ((), (), s32[]{:S(2)}) async-start(), calls=%async_computation.27 | async-start | bytes 786432 | tf_op jit(solution)/shard_map/reduce_scatter | solution.py:47
  516.9 78.7 %reduce-scatter.37.cloned.1.call-start = ((), (), s32[]{:S(2)}) async-start(), calls=%async_computation.26 | async-start | bytes 786432 | tf_op jit(solution)/shard_map/reduce_scatter | solution.py:47
  569.1 49.6 %reduce-scatter.35.cloned.1.call-start = ((), (), s32[]{:S(2)}) async-start(), calls=%async_computation.25 | async-start | bytes 2359296 | tf_op jit(solution)/shard_map/reduce_scatter | solution.py:39
  572.1 84.8 %reduce-scatter.47.cloned.1.call-start = ((), (), s32[]{:S(2)}) async-start(), calls=%async_computation.31 | async-start | bytes 3145728 | tf_op jit(solution)/shard_map/reduce_scatter | solution.py:47
  574.2 120.9 %reduce-scatter.43.cloned.1.call-start = ((), (), s32[]{:S(2)}) async-start(), calls=%async_computation.29 | async-start | bytes 3145728 | tf_op jit(solution)/shard_map/reduce_scatter | solution.py:39
  577.3 149.7 %reduce-scatter.33.cloned.1.call-start = ((), (), s32[]{:S(2)}) async-start(), calls=%async_computation.24 | async-start | bytes 2359296 | tf_op jit(solution)/shard_map/reduce_scatter | solution.py:39
  588.5 176.2 %reduce-scatter.45.cloned.1.call-start = ((), (), s32[]{:S(2)}) async-start(), calls=%async_computation.30 | async-start | bytes 3145728 | tf_op jit(solution)/shard_map/reduce_scatter | solution.py:47
  590.7 212.3 %reduce-scatter.41.cloned.1.call-start = ((), (), s32[]{:S(2)}) async-start(), calls=%async_computation.28 | async-start | bytes 3145728 | tf_op jit(solution)/shard_map/reduce_scatter | solution.py:39
  594.0 369.6 %reduce-scatter.31.cloned.1.call-start = ((), (), s32[]{:S(2)}) async-start(), calls=%async_computation.23 | async-start | bytes 655360 | tf_op jit(solution)/shard_map/reduce_scatter | solution.py:28
  595.5 369.7 %all-reduce.12.cloned.1.call-start = ((), (), s32[]{:S(2)}) async-start(), calls=%async_computation.38 | async-start | bytes 12582912 | tf_op jit(solution)/shard_map/psum | solution.py:34
  (76 other events, 743.2 us)
Sparse Core Ops, SparseCore 0:
  10.3 33.1 all-gather.14
  48.9 29.7 reduce-scatter.16
  81.1 36.4 all-gather.16
  119.2 36.5 all-gather.18
  159.1 29.5 reduce-scatter.18
  190.1 30.6 all-gather.20
  225.9 29.4 reduce-scatter.20
  257.8 36.4 all-gather.22
  296.7 35.9 all-gather.24
  336.2 29.5 reduce-scatter.22
  399.1 29.3 reduce-scatter.24
  461.1 29.2 reduce-scatter.26
  515.8 29.2 reduce-scatter.28
  547.4 18.9 reduce-scatter.38
  569.2 17.5 reduce-scatter.36
  589.1 29.5 reduce-scatter.34
  621.5 35.3 reduce-scatter.46
  659.7 35.3 reduce-scatter.42
  697.4 29.5 reduce-scatter.32
  729.3 35.3 reduce-scatter.44
  767.6 35.3 reduce-scatter.40
  806.3 29.5 reduce-scatter.30
  840.3 123.7 all-reduce.11
where the time goes:
time: 985 us; the launch traced here: 984 us
  waiting for transfers between devices  528 us (54%)
  blocking collectives  314 us (32%)
  matrix products  75 us (8%)
  other arithmetic  29.3 us (3%)
  local copies, waits for them, and re-layouts  21.6 us (2%)
  between operations  15.1 us (2%)
    reduce_scatter x8, waiting for transfers between devices, sum_parts(): lax.psum_scatter(values_in.astype(jnp.bfloat16), 'col', scatter_dimension...  186 us
    psum x1, blocking collectives, shards(): lax.psum((jnp.stack(qv_grads), jnp.stack(outb_grads), jnp.stack(gain_grad...  159 us
    reduce_scatter x4, waiting for transfers between devices, reduce_rows(): lax.psum_scatter(gradient.astype(jnp.bfloat16), 'row', scatter_dimension=...  132 us
    all_gather x8, blocking collectives, gather_features(): return lax.all_gather(values_in, 'col', axis=1, tiled=True)  78.8 us
    reduce_scatter x4, waiting for transfers between devices, reduce_cols(): lax.psum_scatter(gradient.astype(jnp.bfloat16), 'row', scatter_dimension=...  75.8 us
    all_gather x4, waiting for transfers between devices, gather_rows(): return lax.all_gather(weight, 'row', axis=0, tiled=True)  67.4 us
    all_gather x2, waiting for transfers between devices, gather_cols(): return lax.all_gather(weight, 'row', axis=1, tiled=True)  65.7 us
    psum x4, blocking collectives, norm_forward(): lax.psum((jnp.sum(values_in, axis=1), jnp.sum(values_in * values_in, axis...  29.1 us
  transfers between devices with their start and end apart: 23, of which 19 were waited for; matrix products, arithmetic and copies ran while one was open for 6% of the time, Pallas kernels for 0%

commit v1 on v0

v1 whole, which is shorter than its diff:
```python
import functools

import jax
import jax.numpy as jnp
from jax import lax
from jax.experimental import pallas as pl
from jax.experimental.pallas import tpu as pltpu
from jax.sharding import PartitionSpec as P

D = 1024
HD = 64
LAYERS = 2
TOK = 256
OWN = 64
COLS = 256
HEADS_LOCAL = 4
SLABS = 6
EPSILON = 1e-05
MASKED = -1e30
SCALE = HD**-0.5
MESH = pl.DeviceIdType.MESH
BF = jnp.bfloat16
F32 = jnp.float32


def dot(a, b):
    return jnp.dot(a, b, preferred_element_type=F32)


def dot_nt(a, b):
    return lax.dot_general(a, b, (((1,), (1,)), ((), ())), preferred_element_type=F32)


def dot_tn(a, b):
    return lax.dot_general(a, b, (((0,), (0,)), ((), ())), preferred_element_type=F32)


def norm_back(upstream, normed, inverse, gain):
    scaled = upstream * gain
    mean_one = jnp.sum(scaled, axis=1, keepdims=True) / D
    mean_two = jnp.sum(scaled * normed, axis=1, keepdims=True) / D
    return inverse * (scaled - mean_one - normed * mean_two)


def kernel(
    hid, gout, mask, small, upb, qvb, wq, wo, wu, wd,
    hout, gin, gbig, gsmall,
    WQ, WO, WU, WD, PF, A2H, A2G, S, M, U, GS, GF, F1,
    STATE, MID, SEC, FIR, QKV, CTX, PR, DG, ACT, NRM, INV, LL, ML, GC,
    PS, XS, L1, L2, HS, HOB, GIB,
    G, R1, A1, R2, A2, R3, FB,
    SGF, SU, SQ, RC, SM, SZ, SY, SR,
    w_ssem, w_rsem, w_lsem, in_s, in_r, ag_s, ag_r, rs_s, rs_r, gr_s, gr_r, out_s, out_r, lsem, sm_s, sm_r,
):
    dp = lax.axis_index("dp")
    row = lax.axis_index("row")
    col = lax.axis_index("col")
    z, y = lax.div(dp, 4), lax.rem(dp, 4)
    xh, core = lax.div(col, 2), lax.rem(col, 2)
    col_core = xh * 2 + (1 - core)
    col_cross = (1 - xh) * 2 + core
    col_diag = (1 - xh) * 2 + (1 - core)
    core_dev = (dp, row, col_core)
    cross_dev = (dp, row, col_cross)
    row_dev = (dp, 1 - row, col)

    def col_dev(d):
        return (dp, row, lax.rem(col + d, 4))

    def axis_place(axis):
        return z if axis == 0 else y

    def axis_dev(axis, d):
        if axis == 0:
            return (lax.rem(z + d, 4) * 4 + y, row, col)
        return (z * 4 + lax.rem(y + d, 4), row, col)

    def chunk(j, rows=OWN):
        return pl.ds(pl.multiple_of(j * rows, rows), rows)

    def remote(src, dst, ssem, rsem, dev):
        return pltpu.make_async_remote_copy(
            src_ref=src, dst_ref=dst, send_sem=ssem, recv_sem=rsem, device_id=dev, device_id_type=MESH
        )

    barrier = pltpu.get_barrier_semaphore()
    for dev in [col_dev(1), col_dev(2), col_dev(3), row_dev] + [axis_dev(a, d) for a in (0, 1) for d in (1, 2, 3)]:
        pl.semaphore_signal(barrier, 1, device_id=dev, device_id_type=MESH)
    pl.semaphore_wait(barrier, 10)

    def in_copies(d):
        to = lax.rem(col + d, 4)
        dev = (dp, row, to)
        return [
            remote(hid.at[chunk(to)], A2H.at[:, chunk(col, COLS)], in_s.at[0, d - 1], in_r.at[0, d - 1], dev),
            remote(small, PF.at[:, chunk(col, COLS)], in_s.at[1, d - 1], in_r.at[1, d - 1], dev),
            remote(gout.at[chunk(to)], A2G.at[:, chunk(col, COLS)], in_s.at[2, d - 1], in_r.at[2, d - 1], dev),
        ]

    def in_arrivals(d):
        source = lax.rem(col + 4 - d, 4)
        return [
            remote(hid.at[chunk(col)], A2H.at[:, chunk(source, COLS)], in_s.at[0, d - 1], in_r.at[0, d - 1], col_dev(d)),
            remote(small, PF.at[:, chunk(source, COLS)], in_s.at[1, d - 1], in_r.at[1, d - 1], col_dev(d)),
            remote(gout.at[chunk(col)], A2G.at[:, chunk(source, COLS)], in_s.at[2, d - 1], in_r.at[2, d - 1], col_dev(d)),
        ]

    for d in (1, 2, 3):
        for c in in_copies(d):
            c.start()

    pairs = ((wq, WQ), (wo, WO), (wu, WU), (wd, WD))

    def w_local(l, n):
        return pltpu.make_async_copy(pairs[n][0].at[l], pairs[n][1].at[l, row], w_lsem.at[l, n])

    def w_remote(l, n, half):
        return remote(pairs[n][0].at[l], pairs[n][1].at[l, half], w_ssem.at[l, n], w_rsem.at[l, n], row_dev)

    for l in range(LAYERS):
        for n in range(4):
            w_remote(l, n, row).start()
            w_local(l, n).start()

    def w_wait(l, n):
        w_local(l, n).wait()
        w_remote(l, n, 1 - row).wait_recv()

    A2H[:, chunk(col, COLS)] = hid[chunk(col), :]
    A2G[:, chunk(col, COLS)] = gout[chunk(col), :]
    PF[:, chunk(col, COLS)] = small[...]
    for d in (1, 2, 3):
        for c in in_arrivals(d):
            c.wait_recv()
    S[...] = A2H[...].astype(F32)
    U[...] = A2G[...].astype(F32)

    def ag_send(k, X):
        out = []
        for p in (0, 1):
            rows = pl.ds(pl.multiple_of(col * OWN + p * 32, 32), 32)
            out.append(remote(X.at[rows], X.at[rows], ag_s.at[k, p], ag_r.at[k, p], cross_dev))
        out.append(remote(X.at[chunk(col)], X.at[chunk(col)], ag_s.at[k, 2], ag_r.at[k, 2], core_dev))
        return out

    def ag_forward(k, X, p):
        rows = pl.ds(pl.multiple_of(col_cross * OWN + p * 32, 32), 32)
        return remote(X.at[rows], X.at[rows], ag_s.at[k, 3 + p], ag_r.at[k, 3 + p], core_dev)

    def ag_start(k, X):
        for c in ag_send(k, X):
            c.start()

    def ag_finish(k, X):
        for p in (0, 1):
            rows = pl.ds(pl.multiple_of(col_cross * OWN + p * 32, 32), 32)
            remote(X.at[rows], X.at[rows], ag_s.at[k, p], ag_r.at[k, p], cross_dev).wait_recv()
            ag_forward(k, X, p).start()
        remote(X.at[chunk(col_core)], X.at[chunk(col_core)], ag_s.at[k, 2], ag_r.at[k, 2], core_dev).wait_recv()
        for p in (0, 1):
            rows = pl.ds(pl.multiple_of(col_diag * OWN + p * 32, 32), 32)
            remote(X.at[rows], X.at[rows], ag_s.at[k, 3 + p], ag_r.at[k, 3 + p], core_dev).wait_recv()

    def ag_drain(k, X):
        for c in ag_send(k, X):
            c.wait_send()
        for p in (0, 1):
            ag_forward(k, X, p).wait_send()

    def half(h):
        return pl.ds(h * 512, 512)

    def rs_first(k, par, h, t):
        to = (1 - xh) * 2 + (1 - core) if t == 0 else col_core
        return remote(
            PS.at[chunk(to), half(h)], L1.at[par, t, :, half(h)], rs_s.at[k, h * 3 + t], rs_r.at[k, h * 3 + t], core_dev
        )

    def rs_cross(k, par, h):
        return remote(XS.at[:, half(h)], L2.at[par, :, half(h)], rs_s.at[k, h * 3 + 2], rs_r.at[k, h * 3 + 2], cross_dev)

    def rs_send(k, par, h):
        for t in (0, 1):
            rs_first(k, par, h, t).start()

    def rs_mid(k, par, h):
        rs_first(k, par, h, 0).wait_recv()
        total = PS[chunk(col_cross), half(h)].astype(F32) + L1[par, 0, :, half(h)].astype(F32)
        XS[:, half(h)] = total.astype(BF)
        rs_cross(k, par, h).start()

    def rs_end(k, par, h):
        rs_first(k, par, h, 1).wait_recv()
        total = PS[chunk(col), half(h)].astype(F32) + L1[par, 1, :, half(h)].astype(F32)
        rs_cross(k, par, h).wait_recv()
        return total + L2[par, :, half(h)].astype(F32)

    def rs_drain(k, par):
        for h in (0, 1):
            for t in (0, 1):
                rs_first(k, par, h, t).wait_send()
            rs_cross(k, par, h).wait_send()

    def gr_one(l, s, d):
        axis = s % 2
        to = lax.rem(axis_place(axis) + d, 4)
        return remote(
            G.at[l, s, :, chunk(to, 128), :], R1.at[l, s, d - 1], gr_s.at[l, s, d - 1], gr_r.at[l, s, d - 1], axis_dev(axis, d)
        )

    def gr_two(l, s, d):
        axis = 1 - s % 2
        to = lax.rem(axis_place(axis) + d, 4)
        return remote(
            A1.at[l, s, :, chunk(to, 32), :], R2.at[l, s, d - 1], gr_s.at[l, s, 2 + d], gr_r.at[l, s, 2 + d], axis_dev(axis, d)
        )

    def gr_row(l, s):
        return remote(A2.at[l, s, 1 - row], R3.at[l, s], gr_s.at[l, s, 6], gr_r.at[l, s, 6], row_dev)

    def gr_four(l, s, d, place):
        axis = 1 - s % 2
        rows = FB.at[l, s, chunk(place, 32), :]
        return remote(rows, rows, gr_s.at[l, s, 6 + d], gr_r.at[l, s, 6 + d], axis_dev(axis, d))

    def gr_five(l, s, d, place):
        axis = s % 2
        return remote(
            FB.at[l, s], gbig.at[l, s, chunk(place, 128), :], gr_s.at[l, s, 9 + d], gr_r.at[l, s, 9 + d], axis_dev(axis, d)
        )

    def gr_local(l, s):
        return pltpu.make_async_copy(FB.at[l, s], gbig.at[l, s, chunk(axis_place(s % 2), 128), :], lsem.at[l, s])

    def t1(l, s):
        for d in (1, 2, 3):
            gr_one(l, s, d).start()

    def t2(l, s):
        for d in (1, 2, 3):
            gr_one(l, s, d).wait_recv()
        own = chunk(axis_place(s % 2), 128)
        for r in (0, 1):
            total = G[l, s, r, own, :].astype(F32)
            for d in (0, 1, 2):
                total = total + R1[l, s, d, r].astype(F32)
            A1[l, s, r] = total.astype(BF)
        for d in (1, 2, 3):
            gr_two(l, s, d).start()

    def t3(l, s):
        for d in (1, 2, 3):
            gr_two(l, s, d).wait_recv()
        own = chunk(axis_place(1 - s % 2), 32)
        for r in (0, 1):
            total = A1[l, s, r, own, :].astype(F32)
            for d in (0, 1, 2):
                total = total + R2[l, s, d, r].astype(F32)
            A2[l, s, r] = total.astype(BF)
        gr_row(l, s).start()

    def t4(l, s):
        gr_row(l, s).wait_recv()
        place = axis_place(1 - s % 2)
        FB[l, s, chunk(place, 32), :] = (A2[l, s, row].astype(F32) + R3[l, s].astype(F32)).astype(BF)
        for d in (1, 2, 3):
            gr_four(l, s, d, place).start()

    def t5(l, s):
        place = axis_place(1 - s % 2)
        for d in (1, 2, 3):
            gr_four(l, s, d, lax.rem(place + 4 - d, 4)).wait_recv()
        own = axis_place(s % 2)
        for d in (1, 2, 3):
            gr_five(l, s, d, own).start()
        gr_local(l, s).start()

    def t6(l, s):
        own = axis_place(s % 2)
        for d in (1, 2, 3):
            gr_five(l, s, d, lax.rem(own + 4 - d, 4)).wait_recv()
        gr_local(l, s).wait()
        place = axis_place(1 - s % 2)
        for d in (1, 2, 3):
            gr_one(l, s, d).wait_send()
            gr_two(l, s, d).wait_send()
            gr_four(l, s, d, place).wait_send()
            gr_five(l, s, d, own).wait_send()
        gr_row(l, s).wait_send()

    def both(step, l, first):
        step(l, first)
        step(l, first + 1)

    def vec(l, r):
        return PF[pl.ds(l * 8 + r, 1), :]

    def norm_into(values, l, n, gain, shift):
        mean_row = jnp.sum(values, axis=1, keepdims=True) / D
        squares = jnp.sum(values * values, axis=1, keepdims=True) / D
        inverse = lax.rsqrt(squares - mean_row * mean_row + EPSILON)
        normed = (values - mean_row) * inverse
        NRM[l, n] = normed
        INV[l, n] = jnp.broadcast_to(inverse, (OWN, 128))
        return normed * gain + shift

    def forward(l, carry):
        X = STATE.at[l]
        X[chunk(col), :] = S[...].astype(BF)
        ag_start(l * 4, X)
        w_wait(l, 0)
        ag_finish(l * 4, X)
        for j in range(3):
            lanes = pl.ds(j * COLS, COLS)
            mixed = dot(STATE[l, :, :512], WQ[l, 0, :, lanes]) + dot(STATE[l, :, 512:], WQ[l, 1, :, lanes])
            if j != 1:
                mixed = mixed + qvb[l, j // 2 : j // 2 + 1, :]
            QKV[l, j] = mixed.astype(BF)
        ag_drain(l * 4, X)
        for h in range(HEADS_LOCAL):
            lanes = slice(h * HD, (h + 1) * HD)
            scores = dot_nt(QKV[l, 0, :, lanes], QKV[l, 1, :, lanes])
            scaled = jnp.where(mask[...] > 0.5, scores * SCALE, MASKED)
            raised = jnp.exp(scaled - jnp.max(scaled, axis=1, keepdims=True))
            probs = raised / jnp.sum(raised, axis=1, keepdims=True)
            PR[l, h] = probs
            CTX[l, :, lanes] = dot(probs.astype(BF), QKV[l, 2, :, lanes]).astype(BF)
        w_wait(l, 1)
        k = l * 4
        for h in (0, 1):
            PS[:, half(h)] = dot(CTX[l], WO[l, h]).astype(BF)
            rs_send(k, 0, h)
        rs_mid(k, 0, 0)
        rs_mid(k, 0, 1)
        for h in (0, 1):
            F1[:, half(h)] = S[:, half(h)] + rs_end(k, 0, h)
        rs_drain(k, 0)
        middle = norm_into(F1[...] + vec(l, 0), l, 0, vec(l, 1), vec(l, 2))
        M[...] = middle
        X = MID.at[l]
        X[chunk(col), :] = middle.astype(BF)
        ag_start(l * 4 + 1, X)
        w_wait(l, 2)
        ag_finish(l * 4 + 1, X)

        def lift(n, c):
            lanes = chunk(n, COLS)
            lifted = dot(MID[l, :, :512], WU[l, 0, :, lanes]) + dot(MID[l, :, 512:], WU[l, 1, :, lanes])
            lifted = lifted + upb[pl.ds(l, 1), lanes]
            phi = 0.5 * (1.0 + lax.erf(lifted * (0.5**0.5)))
            density = jnp.exp(-0.5 * lifted * lifted) * 0.3989422804014327
            DG[l, :, lanes] = phi + lifted * density
            ACT[l, :, lanes] = (lifted * phi).astype(BF)
            return c

        lax.fori_loop(0, 4, lift, 0)
        ag_drain(l * 4 + 1, X)
        w_wait(l, 3)
        k = l * 4 + 1
        for h in (0, 1):
            for q in (0, 1):
                lanes = pl.ds(h * 512 + q * 256, 256)
                PS[:, lanes] = dot(ACT[l], WD[l, h, :, pl.ds(q * 256, 256)]).astype(BF)
            rs_send(k, 1, h)
        rs_mid(k, 1, 0)
        rs_mid(k, 1, 1)
        for h in (0, 1):
            F1[:, half(h)] = M[:, half(h)] + rs_end(k, 1, h)
        rs_drain(k, 1)
        S[...] = norm_into(F1[...] + vec(l, 5), l, 1, vec(l, 3), vec(l, 4))
        return carry

    lax.fori_loop(0, LAYERS, forward, 0)

    def out_copies(n, d):
        buf = (HOB, GIB)[n]
        to = lax.rem(col + d, 4)
        return remote(
            HS.at[n, :, chunk(to, COLS)], buf.at[chunk(col)], out_s.at[n, d - 1], out_r.at[n, d - 1], (dp, row, to)
        )

    def out_arrivals(n, d):
        buf = (HOB, GIB)[n]
        source = lax.rem(col + 4 - d, 4)
        return remote(
            HS.at[n, :, chunk(col, COLS)], buf.at[chunk(source)], out_s.at[n, d - 1], out_r.at[n, d - 1], col_dev(d)
        )

    HS[0] = S[...].astype(BF)
    for d in (1, 2, 3):
        out_copies(0, d).start()
    HOB[chunk(col), :] = HS[0, :, chunk(col, COLS)]

    def backward(i, carry):
        l = LAYERS - 1 - i
        prev = l + 1
        upstream = U[...]
        normed = NRM[l, 1]
        SGF[l, 3:4, :] = jnp.sum(upstream * normed, axis=0, keepdims=True)
        SGF[l, 4:5, :] = jnp.sum(upstream, axis=0, keepdims=True)
        grad_second = norm_back(upstream, normed, INV[l, 1, :, :1], vec(l, 3))
        GS[...] = grad_second
        SGF[l, 5:6, :] = jnp.sum(grad_second, axis=0, keepdims=True)
        SEC[chunk(col), :] = grad_second.astype(BF)
        k = l * 4 + 2
        ag_start(k, SEC)

        @pl.when(i > 0)
        def _():
            both(t2, prev, 2)
            both(t3, prev, 0)

        ag_finish(k, SEC)

        def pull(n, c):
            lanes = chunk(n, COLS)
            grad_act = dot_nt(SEC[:, :512], WD[l, 0, lanes, :]) + dot_nt(SEC[:, 512:], WD[l, 1, lanes, :])
            grad_lifted = grad_act * DG[l, :, lanes]
            SU[l, :, lanes] = jnp.sum(grad_lifted, axis=0, keepdims=True)
            LL[:, lanes] = grad_lifted.astype(BF)
            return c

        lax.fori_loop(0, 4, pull, 0)
        for h in (0, 1):
            for q in (0, 1):
                lanes = pl.ds(h * 512 + q * 256, 256)
                PS[:, lanes] = dot_nt(LL[...], WU[l, h, pl.ds(q * 256, 256), :]).astype(BF)
            rs_send(k, 0, h)
        rs_mid(k, 0, 0)
        rs_mid(k, 0, 1)

        def down_grad(f, c):
            total = dot_tn(ACT[l, :, chunk(f, COLS)], SEC[...]).astype(BF)
            rows = chunk(lax.rem(f, 2), COLS)
            for r in (0, 1):
                G[l, lax.div(f, 2), r, rows, :] = total[:, r * 512 : (r + 1) * 512]
            return c

        lax.fori_loop(0, 4, down_grad, 0)
        both(t1, l, 0)
        ag_drain(k, SEC)

        @pl.when(i > 0)
        def _():
            both(t2, prev, 4)
            both(t3, prev, 2)
            both(t4, prev, 0)

        for h in (0, 1):
            GS[:, half(h)] = GS[:, half(h)] + rs_end(k, 0, h)
        rs_drain(k, 0)
        grad_middle = GS[...]
        normed = NRM[l, 0]
        SGF[l, 1:2, :] = jnp.sum(grad_middle * normed, axis=0, keepdims=True)
        SGF[l, 2:3, :] = jnp.sum(grad_middle, axis=0, keepdims=True)
        grad_first = norm_back(grad_middle, normed, INV[l, 0, :, :1], vec(l, 1))
        GF[...] = grad_first
        SGF[l, 0:1, :] = jnp.sum(grad_first, axis=0, keepdims=True)
        FIR[chunk(col), :] = grad_first.astype(BF)
        k = l * 4 + 3
        ag_start(k, FIR)

        def up_grad(n, c):
            total = dot_tn(MID[l, :, chunk(n, COLS)], LL[...]).astype(BF)
            rows = chunk(lax.rem(n, 2), COLS)
            for r in (0, 1):
                G[l, 2 + r, lax.div(n, 2), rows, :] = total[:, r * 512 : (r + 1) * 512]
            return c

        lax.fori_loop(0, 4, up_grad, 0)
        both(t1, l, 2)

        @pl.when(i > 0)
        def _():
            both(t3, prev, 4)
            both(t4, prev, 2)
            both(t5, prev, 0)

        ag_finish(k, FIR)
        GC[...] = (dot_nt(FIR[:, :512], WO[l, 0]) + dot_nt(FIR[:, 512:], WO[l, 1])).astype(BF)
        for h in range(HEADS_LOCAL):
            lanes = slice(h * HD, (h + 1) * HD)
            probs = PR[l, h]
            grad_probs = dot_nt(GC[:, lanes], QKV[l, 2, :, lanes])
            centre = jnp.sum(probs * grad_probs, axis=1, keepdims=True)
            grad_scores = (probs * (grad_probs - centre) * SCALE).astype(BF)
            grad_query = dot(grad_scores, QKV[l, 1, :, lanes])
            grad_key = dot_tn(grad_scores, QKV[l, 0, :, lanes])
            grad_value = dot_tn(probs.astype(BF), GC[:, lanes])
            SQ[l, 0:1, lanes] = jnp.sum(grad_query, axis=0, keepdims=True)
            SQ[l, 1:2, lanes] = jnp.sum(grad_value, axis=0, keepdims=True)
            ML[:, h * HD : (h + 1) * HD] = grad_query.astype(BF)
            ML[:, COLS + h * HD : COLS + (h + 1) * HD] = grad_key.astype(BF)
            ML[:, 2 * COLS + h * HD : 2 * COLS + (h + 1) * HD] = grad_value.astype(BF)
        for h in (0, 1):
            for q in (0, 1):
                lanes = pl.ds(h * 512 + q * 256, 256)
                PS[:, lanes] = dot_nt(ML[...], WQ[l, h, pl.ds(q * 256, 256), :]).astype(BF)
            rs_send(k, 1, h)
        rs_mid(k, 1, 0)
        rs_mid(k, 1, 1)
        total = dot_tn(CTX[l], FIR[...]).astype(BF)
        for r in (0, 1):
            G[l, 5, r, 0:256, :] = total[:, r * 512 : (r + 1) * 512]

        def qkv_grad(r, c):
            for q in (0, 1):
                total = dot_tn(STATE[l, :, chunk(2 * r + q, COLS)], ML[...]).astype(BF)
                G[l, 4, r, q * 256 : (q + 1) * 256, :] = total[:, :512]
                G[l, 5, r, 256:512, q * 256 : (q + 1) * 256] = total[:, 512:]
            return c

        lax.fori_loop(0, 2, qkv_grad, 0)
        both(t1, l, 4)
        ag_drain(k, FIR)
        both(t2, l, 0)

        @pl.when(i > 0)
        def _():
            both(t4, prev, 4)
            both(t5, prev, 2)

        for h in (0, 1):
            U[:, half(h)] = GF[:, half(h)] + rs_end(k, 1, h)
        rs_drain(k, 1)
        return carry

    lax.fori_loop(0, LAYERS, backward, 0)

    HS[1] = U[...].astype(BF)
    for d in (1, 2, 3):
        out_copies(1, d).start()
    GIB[chunk(col), :] = HS[1, :, chunk(col, COLS)]

    def sc_copy(d):
        to = lax.rem(col + d, 4)
        return remote(SGF.at[:, :, chunk(to, COLS)], RC.at[d - 1], sm_s.at[0, d - 1], sm_r.at[0, d - 1], (dp, row, to))

    def sd_copy(axis, d, place):
        buf = (SZ, SY)[axis]
        return remote(
            buf.at[axis_place(axis)], buf.at[place], sm_s.at[1 + axis, d - 1], sm_r.at[1 + axis, d - 1], axis_dev(axis, d)
        )

    def sr_copy():
        return remote(SM, SR, sm_s.at[3, 0], sm_r.at[3, 0], row_dev)

    for d in (1, 2, 3):
        sc_copy(d).start()
    both(t2, 0, 2)
    both(t3, 0, 0)
    both(t5, 1, 4)
    for d in (1, 2, 3):
        sc_copy(d).wait_recv()
    feature = SGF[:, :, chunk(col, COLS)]
    for d in (0, 1, 2):
        feature = feature + RC[d]
    for l in range(LAYERS):
        SZ[z, 8 * l : 8 * l + 8, :] = feature[l]
        for q in range(4):
            SZ[z, 16 + 4 * l + q : 17 + 4 * l + q, :] = SU[l, :, q * COLS : (q + 1) * COLS]
        SZ[z, 24 + 2 * l : 26 + 2 * l, :] = SQ[l]
    SZ[z, 28:32, :] = jnp.zeros((4, COLS), F32)
    for d in (1, 2, 3):
        sd_copy(0, d, z).start()
    both(t2, 0, 4)
    both(t3, 0, 2)
    both(t4, 0, 0)
    for d in (1, 2, 3):
        sd_copy(0, d, lax.rem(z + 4 - d, 4)).wait_recv()
    SY[y] = SZ[0] + SZ[1] + SZ[2] + SZ[3]
    for d in (1, 2, 3):
        sd_copy(1, d, y).start()
    both(t3, 0, 4)
    both(t4, 0, 2)
    both(t5, 0, 0)
    for d in (1, 2, 3):
        sd_copy(1, d, lax.rem(y + 4 - d, 4)).wait_recv()
    SM[...] = SY[0] + SY[1] + SY[2] + SY[3]
    sr_copy().start()
    both(t4, 0, 4)
    both(t5, 0, 2)
    sr_copy().wait_recv()
    gsmall[...] = SM[...] + SR[...]
    both(t5, 0, 4)

    for n in (0, 1):
        for d in (1, 2, 3):
            out_arrivals(n, d).wait_recv()
    hout[...] = HOB[...]
    gin[...] = GIB[...]

    for d in (1, 2, 3):
        for c in in_copies(d):
            c.wait_send()
        for n in (0, 1):
            out_copies(n, d).wait_send()
        sc_copy(d).wait_send()
        sd_copy(0, d, z).wait_send()
        sd_copy(1, d, y).wait_send()
    sr_copy().wait_send()
    for l in range(LAYERS):
        for n in range(4):
            w_remote(l, n, row).wait_send()

    def finish(l, c):
        for s in range(SLABS):
            t6(l, s)
        return c

    lax.fori_loop(0, LAYERS, finish, 0)


def step_call(*args):
    vmem = pl.BlockSpec(memory_space=pltpu.VMEM)
    hbm = pl.BlockSpec(memory_space=pl.ANY)
    dma = pltpu.SemaphoreType.DMA
    V = pltpu.VMEM
    L = LAYERS
    scratch = [
        V((L, 2, 512, 768), BF), V((L, 2, 256, 512), BF), V((L, 2, 512, 1024), BF), V((L, 2, 1024, 512), BF),
        V((16, 1024), F32), V((OWN, D), BF), V((OWN, D), BF),
        V((OWN, D), F32), V((OWN, D), F32), V((OWN, D), F32), V((OWN, D), F32), V((OWN, D), F32), V((OWN, D), F32),
        V((L, TOK, D), BF), V((L, TOK, D), BF), V((TOK, D), BF), V((TOK, D), BF),
        V((L, 3, TOK, COLS), BF), V((L, TOK, COLS), BF), V((L, HEADS_LOCAL, TOK, TOK), F32),
        V((L, TOK, 1024), F32), V((L, TOK, 1024), BF), V((L, 2, OWN, D), F32), V((L, 2, OWN, 128), F32),
        V((TOK, 1024), BF), V((TOK, 768), BF), V((TOK, COLS), BF),
        V((TOK, D), BF), V((OWN, D), BF), V((2, 2, OWN, D), BF), V((2, OWN, D), BF),
        V((2, OWN, D), BF), V((TOK, COLS), BF), V((TOK, COLS), BF),
        V((L, SLABS, 2, 512, 512), BF), V((L, SLABS, 3, 2, 128, 512), BF), V((L, SLABS, 2, 128, 512), BF),
        V((L, SLABS, 3, 2, 32, 512), BF), V((L, SLABS, 2, 32, 512), BF), V((L, SLABS, 32, 512), BF),
        V((L, SLABS, 128, 512), BF),
        V((L, 8, D), F32), V((L, 1, 1024), F32), V((L, 2, COLS), F32), V((3, L, 8, COLS), F32),
        V((32, COLS), F32), V((4, 32, COLS), F32), V((4, 32, COLS), F32), V((32, COLS), F32),
        dma((L, 4)), dma((L, 4)), dma((L, 4)), dma((3, 3)), dma((3, 3)),
        dma((8, 5)), dma((8, 5)), dma((8, 6)), dma((8, 6)),
        dma((L, SLABS, 13)), dma((L, SLABS, 13)), dma((2, 3)), dma((2, 3)), dma((L, SLABS)), dma((4, 3)), dma((4, 3)),
    ]
    return pl.pallas_call(
        kernel,
        out_shape=[
            jax.ShapeDtypeStruct((TOK, COLS), BF),
            jax.ShapeDtypeStruct((TOK, COLS), BF),
            jax.ShapeDtypeStruct((L, SLABS, 512, 512), BF),
            jax.ShapeDtypeStruct((32, COLS), F32),
        ],
        in_specs=[vmem] * 6 + [hbm] * 4,
        out_specs=[vmem, vmem, hbm, vmem],
        scratch_shapes=scratch,
        compiler_params=pltpu.CompilerParams(
            collective_id=0, has_side_effects=True, vmem_limit_bytes=63 * 2**20
        ),
        name="encoder_step",
    )(*args)


def shards(
    hidden_in, seg_ids, key_mask, w_qkv, qv_bias, w_out, out_bias, ln_gain, ln_shift,
    w_up, up_bias, w_down, down_bias, grad_out,
):
    places = jnp.arange(TOK, dtype=jnp.int32)
    allowed = (seg_ids[:, None] == seg_ids[None, :]) & (
        (key_mask[None, :] == 1) | (places[:, None] == places[None, :])
    )
    zero = jnp.zeros((LAYERS, COLS), F32)
    small = jnp.stack(
        [out_bias, ln_gain[:, 0], ln_shift[:, 0], ln_gain[:, 1], ln_shift[:, 1], down_bias, zero, zero], axis=1
    ).reshape(LAYERS * 8, COLS)
    hout, gin, big, sums = step_call(
        hidden_in, grad_out, allowed.astype(F32), small, up_bias, qv_bias,
        w_qkv.reshape(LAYERS, 512, 768), w_out, w_up, w_down,
    )
    big = big.astype(F32)
    grad_down = big[:, 0:2].reshape(LAYERS, 1024, 512)
    grad_up = jnp.concatenate([big[:, 2], big[:, 3]], axis=2)
    value_part = jnp.concatenate([big[:, 5, 256:, :256], big[:, 5, 256:, 256:]], axis=1)
    grad_qkv = jnp.concatenate([big[:, 4], value_part], axis=2).reshape(LAYERS, 512, 3, COLS)
    grad_out_w = big[:, 5, :256]
    feature = sums[:16].reshape(LAYERS, 8, COLS)
    return (
        hout,
        gin,
        grad_qkv,
        sums[24:28].reshape(LAYERS, 2, COLS),
        grad_out_w,
        feature[:, 0],
        jnp.stack([feature[:, 1], feature[:, 3]], axis=1),
        jnp.stack([feature[:, 2], feature[:, 4]], axis=1),
        grad_up,
        sums[16:24].reshape(LAYERS, 1024),
        grad_down,
        feature[:, 5],
    )


def solution(mesh):
    tokens = P(("dp", "row"), "col")
    return jax.shard_map(
        shards,
        mesh=mesh,
        in_specs=(
            tokens, P(("dp", "row")), P(("dp", "row")), P(None, "row", None, "col"), P(None, None, "col"),
            P(None, "col", "row"), P(None, "col"), P(None, None, "col"), P(None, None, "col"),
            P(None, "row", "col"), P(None, "col"), P(None, "col", "row"), P(None, "col"), tokens,
        ),
        out_specs=(
            tokens, tokens, P(None, "row", None, "col"), P(None, None, "col"), P(None, "col", "row"),
            P(None, "col"), P(None, None, "col"), P(None, None, "col"), P(None, "row", "col"),
            P(None, "col"), P(None, "col", "row"), P(None, "col"),
        ),
        check_vma=False,
    )
```

time: 985 us -> 391 us (0.40)
  waiting for transfers between devices: 528 us -> 0 us
  Pallas kernels: 0 us -> 358 us
  blocking collectives: 314 us -> 0 us
  matrix products: 75 us -> 0 us
  other arithmetic: 29.3 us -> 7.71 us
  between operations: 15.1 us -> 0.71 us
    reduce_scatter x16 -> x0, waiting for transfers between devices: 393 us -> none  [the longest x8 186 us: sum_parts(): lax.psum_scatter(values_in.astype(jnp.bfloat16), 'col', scatter_dimension...]
    pallas_call x0 -> x1, Pallas kernels: none -> 358 us  [step_call(): pl.pallas_call(kernel, out_shape=[jax.ShapeDtypeStruct((TOK, COLS), BF),...]
    psum x9 -> x0, blocking collectives: 217 us -> none  [the longest x1 159 us: shards(): lax.psum((jnp.stack(qv_grads), jnp.stack(outb_grads), jnp.stack(gain_grad...]
    all_gather x6 -> x0, waiting for transfers between devices: 133 us -> none  [the longest x4 67.4 us: gather_rows(): return lax.all_gather(weight, 'row', axis=0, tiled=True)]
    all_gather x10 -> x0, blocking collectives: 96 us -> none  [the longest x8 78.8 us: gather_features(): return lax.all_gather(values_in, 'col', axis=1, tiled=True)]
    dot_general x36 -> x0, matrix products: 75 us -> none  [the longest x2 10.9 us: shards(): jnp.dot(middle_full, up_full, preferred_element_type=jnp.float32)]
    reduce_sum x11 -> x0, other arithmetic: 12.6 us -> none  [the longest x4 4.55 us: norm_forward(): jnp.sum(values_in, axis=1)]
  transfers between devices with their start and end apart: 23 -> 0, of which waited for: 19 -> 0; matrix products, arithmetic and copies ran while one was open for 6% -> 0% of each run, Pallas kernels for 0% -> 0%
where the time goes in v1:
time: 391 us; the launch traced here: 390 us
  Pallas kernels  358 us (92%)
  local copies, waits for them, and re-layouts  24.2 us (6%)
  other arithmetic  7.71 us (2%)
    pallas_call x1, Pallas kernels, step_call(): pl.pallas_call(kernel, out_shape=[jax.ShapeDtypeStruct((TOK, COLS), BF),...  358 us

profile of v1, /device:TPU:0, one launch (start us, length us, event | category | flops | bytes accessed | tf_op | source)
XLA Modules:
  0.0 390.3 jit_solution(5069238599303336104)
XLA Ops:
  0.6 0.7 broadcast_compare_fusion
  1.3 0.7 copy.33
  2.0 0.7 copy.34
  2.7 0.8 fusion.4
  3.5 0.6 stack.21
  4.1 1.6 fusion.2.mask
  5.7 1.7 copy.35
  7.4 1.6 copy.36.wq
  9.0 357.7 %encoder_step.1 = (bf16[256,256]{1,0:T(8,128)(2,1)}, bf16[256,256]{1,0:T(8,128)(2,1)}, bf16[2,6,512,512]{3,2,1,0:T(8,128)(2,1)}, f32[32,256]{1,0:T(8,128)}) custom-call(bf16[256,256]{1,0:T(8,128)(2,1)} %hid.1, bf16[256,256]{1,0:T(8,128)(2,1)} %gout.1, f32[256,256]{1,0:T(8,128)} %fusion.2.mask, f32[16,256]{1,0:T(8,128)} %bitcast.33, f32[2,1024]{1,0:T(2,128)} %upb.1, ...), custom_call_target="tpu_custom_call" | custom-call | tf_op jit(solution)/shard_map/encoder_step/pallas_call | solution.py:639
  366.7 0.7 slice.67
  367.4 0.6 reshape.52
  368.0 0.7 slice.77
  368.7 0.7 slice_bitcast_fusion.6
  370.0 0.6 reshape.54
  371.2 0.6 pad_maximum_fusion.2
  372.4 4.3 %slice.91 = f32[2,2,512,512]{3,2,1,0:T(8,128)} slice(bf16[2,6,512,512]{3,2,1,0:T(8,128)(2,1)} %get-tuple-element.18), slice={[0:2], [0:2], [0:512], [0:512]} | slice | bytes 8388608 | tf_op jit(solution)/shard_map/slice | solution.py:674
  376.7 1.7 convert_element_type.7
  378.5 1.0 slice_bitcast_fusion.3
  379.6 0.9 slice_bitcast_fusion.1
  380.5 2.3 pad_maximum_fusion
  383.1 2.3 copy.38
  385.4 3.6 copy.41
  389.0 0.7 copy.52
  389.7 0.7 copy.53
  (13 shorter events, 2.1 us)
Async XLA Ops:
  372.4 4.3 %copy-start = (bf16[2,6,512,512]{3,2,1,0:T(8,128)(2,1)S(1)}, bf16[2,6,512,512]{3,2,1,0:T(8,128)(2,1)}, u32[]{:S(2)}) copy-start(bf16[2,6,512,512]{3,2,1,0:T(8,128)(2,1)} %get-tuple-element.18) | copy-start | bytes 18874372
  385.4 3.6 copy-start.2
  385.4 4.2 %copy-start.1 = (bf16[256,256]{1,0:T(8,128)(2,1)S(1)}, bf16[256,256]{1,0:T(8,128)(2,1)}, u32[]{:S(2)}) copy-start(bf16[256,256]{1,0:T(8,128)(2,1)} %get-tuple-element.74) | copy-start | bytes 393220

commit v2 on v1

--- a/solution.py
+++ b/solution.py
@@ -18,6 +18,9 @@
 EPSILON = 1e-05
 MASKED = -1e30
 SCALE = HD**-0.5
+PARTS = ((0, 1, 2, 0), (0, 2, 3, 1), (1, 128, 512, 0), (2, 256, 640, 0), (2, 640, 1024, 1), (3, 128, 256, 0), (3, 256, 512, 1))
+DIRECT = ((0, 0, 1), (1, 0, 128), (2, 0, 256), (3, 0, 128))
+WEIGHT_ROWS = (512, 256, 512, 1024)
 MESH = pl.DeviceIdType.MESH
 BF = jnp.bfloat16
 F32 = jnp.float32
@@ -43,14 +46,14 @@
 
 
 def kernel(
-    hid, gout, mask, small, upb, qvb, wq, wo, wu, wd,
-    hout, gin, gbig, gsmall,
-    WQ, WO, WU, WD, PF, A2H, A2G, S, M, U, GS, GF, F1,
+    hid, gout, seg, key, outb, gain, shift, downb, upb, qvb, wq, wo, wu, wd,
+    hout, gin, gq, go, gu, gd, gsmall,
+    mask, small, WQ, WO, WU, WD, PF, A2H, A2G, S, M, U, GS, GF, F1,
     STATE, MID, SEC, FIR, QKV, CTX, PR, DG, ACT, NRM, INV, LL, ML, GC,
     PS, XS, L1, L2, HS, HOB, GIB,
     G, R1, A1, R2, A2, R3, FB,
     SGF, SU, SQ, RC, SM, SZ, SY, SR,
-    w_ssem, w_rsem, w_lsem, in_s, in_r, ag_s, ag_r, rs_s, rs_r, gr_s, gr_r, out_s, out_r, lsem, sm_s, sm_r,
+    w_s, w_r, wd_s, wd_r, w_lsem, in_s, in_r, ag_s, ag_r, rs_s, rs_r, gr_s, gr_r, out_s, out_r, lsem, sm_s, sm_r,
 ):
     dp = lax.axis_index("dp")
     row = lax.axis_index("row")
@@ -105,26 +108,119 @@
             remote(gout.at[chunk(col)], A2G.at[:, chunk(source, COLS)], in_s.at[2, d - 1], in_r.at[2, d - 1], col_dev(d)),
         ]
 
-    for d in (1, 2, 3):
-        for c in in_copies(d):
+    for l in range(LAYERS):
+        rows = (outb[l : l + 1], gain[l, 0:1], shift[l, 0:1], gain[l, 1:2], shift[l, 1:2], downb[l : l + 1])
+        for r in range(6):
+            small[l * 8 + r : l * 8 + r + 1, :] = rows[r]
+        small[l * 8 + 6 : l * 8 + 8, :] = jnp.zeros((2, COLS), F32)
+    for d in (1, 2, 3):
+        for c in in_copies(d)[:2]:
             c.start()
 
     pairs = ((wq, WQ), (wo, WO), (wu, WU), (wd, WD))
+
+    def region(ref, n, lo, hi, rows):
+        if n == 0:
+            return ref.at[lo, rows, :]
+        return ref.at[rows, pl.ds(lo, hi - lo)]
 
     def w_local(l, n):
         return pltpu.make_async_copy(pairs[n][0].at[l], pairs[n][1].at[l, row], w_lsem.at[l, n])
 
-    def w_remote(l, n, half):
-        return remote(pairs[n][0].at[l], pairs[n][1].at[l, half], w_ssem.at[l, n], w_rsem.at[l, n], row_dev)
-
+    def w_direct(l, n, which):
+        rows = pl.ds(0, WEIGHT_ROWS[n])
+        _, lo, hi = DIRECT[n]
+        return remote(
+            region(pairs[n][0].at[l], n, lo, hi, rows), region(pairs[n][1].at[l, which], n, lo, hi, rows),
+            wd_s.at[l, n], wd_r.at[l, n], row_dev,
+        )
+
+    def part_axes(p):
+        first = PARTS[p][3]
+        return first, 1 - first
+
+    def part_rows(p, a_place, b_place):
+        piece = WEIGHT_ROWS[PARTS[p][0]] // 16
+        return pl.ds(pl.multiple_of((b_place * 4 + a_place) * piece, piece), piece)
+
+    def w_piece(l, p, which):
+        n, lo, hi, _ = PARTS[p]
+        first, second = part_axes(p)
+        rows = part_rows(p, axis_place(first), axis_place(second))
+        return remote(
+            region(pairs[n][0].at[l], n, lo, hi, rows), region(pairs[n][1].at[l, which], n, lo, hi, rows),
+            w_s.at[l, p, 0], w_r.at[l, p, 0], row_dev,
+        )
+
+    def w_one(l, p, d, place):
+        n, lo, hi, _ = PARTS[p]
+        first, second = part_axes(p)
+        rows = part_rows(p, place, axis_place(second))
+        ref = region(pairs[n][1].at[l, 1 - row], n, lo, hi, rows)
+        return remote(ref, ref, w_s.at[l, p, d], w_r.at[l, p, d], axis_dev(first, d))
+
+    def w_two(l, p, d, place):
+        n, lo, hi, _ = PARTS[p]
+        _, second = part_axes(p)
+        block = WEIGHT_ROWS[n] // 4
+        ref = region(pairs[n][1].at[l, 1 - row], n, lo, hi, chunk(place, block))
+        return remote(ref, ref, w_s.at[l, p, 3 + d], w_r.at[l, p, 3 + d], axis_dev(second, d))
+
+    def back(place, d):
+        return lax.rem(place + 4 - d, 4)
+
+    def w_step_one(l, p):
+        w_piece(l, p, 1 - row).wait_recv()
+        for d in (1, 2, 3):
+            w_one(l, p, d, axis_place(part_axes(p)[0])).start()
+
+    def w_step_two(l, p):
+        first, second = part_axes(p)
+        for d in (1, 2, 3):
+            w_one(l, p, d, back(axis_place(first), d)).wait_recv()
+        for d in (1, 2, 3):
+            w_two(l, p, d, axis_place(second)).start()
+
+    def w_wait(l, n):
+        w_local(l, n).wait()
+        w_direct(l, n, 1 - row).wait_recv()
+        for p in range(len(PARTS)):
+            if PARTS[p][0] == n:
+                second = part_axes(p)[1]
+                for d in (1, 2, 3):
+                    w_two(l, p, d, back(axis_place(second), d)).wait_recv()
+
+    def w_drain(l):
+        for n in range(4):
+            w_direct(l, n, row).wait_send()
+        for p in range(len(PARTS)):
+            first, second = part_axes(p)
+            w_piece(l, p, row).wait_send()
+            for d in (1, 2, 3):
+                w_one(l, p, d, axis_place(first)).wait_send()
+                w_two(l, p, d, axis_place(second)).wait_send()
+
+    parts = range(len(PARTS))
+    for p in parts:
+        w_piece(0, p, row).start()
+    w_direct(0, 0, row).start()
+    for d in (1, 2, 3):
+        in_copies(d)[2].start()
+    for p in parts:
+        w_piece(1, p, row).start()
     for l in range(LAYERS):
         for n in range(4):
-            w_remote(l, n, row).start()
             w_local(l, n).start()
-
-    def w_wait(l, n):
-        w_local(l, n).wait()
-        w_remote(l, n, 1 - row).wait_recv()
+            if l + n > 0:
+                w_direct(l, n, row).start()
+    for p in parts:
+        w_step_one(0, p)
+
+    seg_lanes = jnp.broadcast_to(seg[...].astype(F32), (TOK, TOK))
+    key_lanes = jnp.broadcast_to(key[...].astype(F32), (TOK, TOK))
+    same_place = lax.broadcasted_iota(jnp.int32, (TOK, TOK), 0) == lax.broadcasted_iota(jnp.int32, (TOK, TOK), 1)
+    keep = jnp.where(same_place, 1.0, key_lanes)
+    mask[...] = jnp.where(seg_lanes.T == seg_lanes, keep, 0.0)
 
     A2H[:, chunk(col, COLS)] = hid[chunk(col), :]
     A2G[:, chunk(col, COLS)] = gout[chunk(col), :]
@@ -134,6 +230,8 @@
             c.wait_recv()
     S[...] = A2H[...].astype(F32)
     U[...] = A2G[...].astype(F32)
+    w_step_two(0, 0)
+    w_step_two(0, 1)
 
     def ag_send(k, X):
         out = []
@@ -223,14 +321,34 @@
         rows = FB.at[l, s, chunk(place, 32), :]
         return remote(rows, rows, gr_s.at[l, s, 6 + d], gr_r.at[l, s, 6 + d], axis_dev(axis, d))
 
+    def places(l, s, place):
+        if s < 2:
+            return [(pl.ds(0, 128), pl.ds(0, 512), gd.at[l, pl.ds(pl.multiple_of(s * 512 + place * 128, 128), 128), :])]
+        if s < 4:
+            return [(pl.ds(0, 128), pl.ds(0, 512), gu.at[l, chunk(place, 128), pl.ds((s - 2) * 512, 512)])]
+        if s == 4:
+            return [(pl.ds(0, 128), pl.ds(j * COLS, COLS), gq.at[l, j, chunk(place, 128), :]) for j in (0, 1)]
+        return [
+            (pl.ds(0, 64), pl.ds(0, 512), go.at[l, chunk(place, 64), :]),
+            (pl.ds(64, 64), pl.ds(0, COLS), gq.at[l, 2, chunk(place, 64), :]),
+            (pl.ds(64, 64), pl.ds(COLS, COLS), gq.at[l, 2, pl.ds(pl.multiple_of(256 + place * 64, 64), 64), :]),
+        ]
+
     def gr_five(l, s, d, place):
         axis = s % 2
-        return remote(
-            FB.at[l, s], gbig.at[l, s, chunk(place, 128), :], gr_s.at[l, s, 9 + d], gr_r.at[l, s, 9 + d], axis_dev(axis, d)
-        )
+        return [
+            remote(
+                FB.at[l, s, rows, lanes], to, gr_s.at[l, s, 6 + 3 * d + q + 1], gr_r.at[l, s, 6 + 3 * d + q + 1],
+                axis_dev(axis, d),
+            )
+            for q, (rows, lanes, to) in enumerate(places(l, s, place))
+        ]
 
     def gr_local(l, s):
-        return pltpu.make_async_copy(FB.at[l, s], gbig.at[l, s, chunk(axis_place(s % 2), 128), :], lsem.at[l, s])
+        return [
+            pltpu.make_async_copy(FB.at[l, s, rows, lanes], to, lsem.at[l, s, q])
+            for q, (rows, lanes, to) in enumerate(places(l, s, axis_place(s % 2)))
+        ]
 
     def t1(l, s):
         for d in (1, 2, 3):
@@ -272,20 +390,25 @@
             gr_four(l, s, d, lax.rem(place + 4 - d, 4)).wait_recv()
         own = axis_place(s % 2)
         for d in (1, 2, 3):
-            gr_five(l, s, d, own).start()
-        gr_local(l, s).start()
+            for c in gr_five(l, s, d, own):
+                c.start()
+        for c in gr_local(l, s):
+            c.start()
 
     def t6(l, s):
         own = axis_place(s % 2)
         for d in (1, 2, 3):
-            gr_five(l, s, d, lax.rem(own + 4 - d, 4)).wait_recv()
-        gr_local(l, s).wait()
+            for c in gr_five(l, s, d, lax.rem(own + 4 - d, 4)):
+                c.wait_recv()
+        for c in gr_local(l, s):
+            c.wait()
         place = axis_place(1 - s % 2)
         for d in (1, 2, 3):
             gr_one(l, s, d).wait_send()
             gr_two(l, s, d).wait_send()
             gr_four(l, s, d, place).wait_send()
-            gr_five(l, s, d, own).wait_send()
+            for c in gr_five(l, s, d, own):
+                c.wait_send()
         gr_row(l, s).wait_send()
 
     def both(step, l, first):
@@ -308,11 +431,18 @@
         X = STATE.at[l]
         X[chunk(col), :] = S[...].astype(BF)
         ag_start(l * 4, X)
+
+        @pl.when(l == 0)
+        def _():
+            for p in parts[2:]:
+                w_step_two(0, p)
+            for p in parts:
+                w_step_one(1, p)
+
         w_wait(l, 0)
         ag_finish(l * 4, X)
         for j in range(3):
-            lanes = pl.ds(j * COLS, COLS)
-            mixed = dot(STATE[l, :, :512], WQ[l, 0, :, lanes]) + dot(STATE[l, :, 512:], WQ[l, 1, :, lanes])
+            mixed = dot(STATE[l, :, :512], WQ[l, 0, j]) + dot(STATE[l, :, 512:], WQ[l, 1, j])
             if j != 1:
                 mixed = mixed + qvb[l, j // 2 : j // 2 + 1, :]
             QKV[l, j] = mixed.astype(BF)
@@ -325,6 +455,12 @@
             probs = raised / jnp.sum(raised, axis=1, keepdims=True)
             PR[l, h] = probs
             CTX[l, :, lanes] = dot(probs.astype(BF), QKV[l, 2, :, lanes]).astype(BF)
+
+        @pl.when(l == 0)
+        def _():
+            for p in parts:
+                w_step_two(1, p)
+
         w_wait(l, 1)
         k = l * 4
         for h in (0, 1):
@@ -495,19 +631,23 @@
         for h in (0, 1):
             for q in (0, 1):
                 lanes = pl.ds(h * 512 + q * 256, 256)
-                PS[:, lanes] = dot_nt(ML[...], WQ[l, h, pl.ds(q * 256, 256), :]).astype(BF)
+                PS[:, lanes] = sum(
+                    dot_nt(ML[:, j * COLS : (j + 1) * COLS], WQ[l, h, j, pl.ds(q * 256, 256), :]) for j in range(3)
+                ).astype(BF)
             rs_send(k, 1, h)
         rs_mid(k, 1, 0)
         rs_mid(k, 1, 1)
         total = dot_tn(CTX[l], FIR[...]).astype(BF)
         for r in (0, 1):
-            G[l, 5, r, 0:256, :] = total[:, r * 512 : (r + 1) * 512]
+            for q in range(4):
+                G[l, 5, r, q * 128 : q * 128 + 64, :] = total[q * 64 : (q + 1) * 64, r * 512 : (r + 1) * 512]
 
         def qkv_grad(r, c):
             for q in (0, 1):
                 total = dot_tn(STATE[l, :, chunk(2 * r + q, COLS)], ML[...]).astype(BF)
                 G[l, 4, r, q * 256 : (q + 1) * 256, :] = total[:, :512]
-                G[l, 5, r, 256:512, q * 256 : (q + 1) * 256] = total[:, 512:]
+                for b in range(4):
+                    G[l, 5, r, b * 128 + 64 : b * 128 + 128, q * 256 : (q + 1) * 256] = total[b * 64 : (b + 1) * 64, 512:]
             return c
 
         lax.fori_loop(0, 2, qkv_grad, 0)
@@ -600,8 +740,7 @@
         sd_copy(1, d, y).wait_send()
     sr_copy().wait_send()
     for l in range(LAYERS):
-        for n in range(4):
-            w_remote(l, n, row).wait_send()
+        w_drain(l)
 
     def finish(l, c):
         for s in range(SLABS):
@@ -618,7 +757,8 @@
     V = pltpu.VMEM
     L = LAYERS
     scratch = [
-        V((L, 2, 512, 768), BF), V((L, 2, 256, 512), BF), V((L, 2, 512, 1024), BF), V((L, 2, 1024, 512), BF),
+        V((TOK, TOK), F32), V((16, COLS), F32),
+        V((L, 2, 3, 512, COLS), BF), V((L, 2, 256, 512), BF), V((L, 2, 512, 1024), BF), V((L, 2, 1024, 512), BF),
         V((16, 1024), F32), V((OWN, D), BF), V((OWN, D), BF),
         V((OWN, D), F32), V((OWN, D), F32), V((OWN, D), F32), V((OWN, D), F32), V((OWN, D), F32), V((OWN, D), F32),
         V((L, TOK, D), BF), V((L, TOK, D), BF), V((TOK, D), BF), V((TOK, D), BF),
@@ -632,20 +772,23 @@
         V((L, SLABS, 128, 512), BF),
         V((L, 8, D), F32), V((L, 1, 1024), F32), V((L, 2, COLS), F32), V((3, L, 8, COLS), F32),
         V((32, COLS), F32), V((4, 32, COLS), F32), V((4, 32, COLS), F32), V((32, COLS), F32),
-        dma((L, 4)), dma((L, 4)), dma((L, 4)), dma((3, 3)), dma((3, 3)),
+        dma((L, 7, 7)), dma((L, 7, 7)), dma((L, 4)), dma((L, 4)), dma((L, 4)), dma((3, 3)), dma((3, 3)),
         dma((8, 5)), dma((8, 5)), dma((8, 6)), dma((8, 6)),
-        dma((L, SLABS, 13)), dma((L, SLABS, 13)), dma((2, 3)), dma((2, 3)), dma((L, SLABS)), dma((4, 3)), dma((4, 3)),
+        dma((L, SLABS, 19)), dma((L, SLABS, 19)), dma((2, 3)), dma((2, 3)), dma((L, SLABS, 3)), dma((4, 3)), dma((4, 3)),
     ]
     return pl.pallas_call(
         kernel,
         out_shape=[
             jax.ShapeDtypeStruct((TOK, COLS), BF),
             jax.ShapeDtypeStruct((TOK, COLS), BF),
-            jax.ShapeDtypeStruct((L, SLABS, 512, 512), BF),
+            jax.ShapeDtypeStruct((L, 3, 512, COLS), BF),
+            jax.ShapeDtypeStruct((L, 256, 512), BF),
+            jax.ShapeDtypeStruct((L, 512, 1024), BF),
+            jax.ShapeDtypeStruct((L, 1024, 512), BF),
             jax.ShapeDtypeStruct((32, COLS), F32),
         ],
-        in_specs=[vmem] * 6 + [hbm] * 4,
-        out_specs=[vmem, vmem, hbm, vmem],
+        in_specs=[vmem] * 10 + [hbm] * 4,
+        out_specs=[vmem, vmem, hbm, hbm, hbm, hbm, vmem],
         scratch_shapes=scratch,
         compiler_params=pltpu.CompilerParams(
             collective_id=0, has_side_effects=True, vmem_limit_bytes=63 * 2**20
@@ -654,42 +797,54 @@
     )(*args)
 
 
+def split_small(hout, gin, sums, out_h, out_g, qvb, outb, gain, shift, upb, downb):
+    out_h[...] = hout[...]
+    out_g[...] = gin[...]
+    for l in range(LAYERS):
+        outb[l : l + 1, :] = sums[8 * l : 8 * l + 1, :]
+        for n in (0, 1):
+            gain[l, n : n + 1, :] = sums[8 * l + 1 + 2 * n : 8 * l + 2 + 2 * n, :]
+            shift[l, n : n + 1, :] = sums[8 * l + 2 + 2 * n : 8 * l + 3 + 2 * n, :]
+        downb[l : l + 1, :] = sums[8 * l + 5 : 8 * l + 6, :]
+        for q in range(4):
+            upb[l : l + 1, q * COLS : (q + 1) * COLS] = sums[16 + 4 * l + q : 17 + 4 * l + q, :]
+        qvb[l] = sums[24 + 2 * l : 26 + 2 * l, :]
+
+
+def split_call(hout, gin, sums):
+    vmem = pl.BlockSpec(memory_space=pltpu.VMEM)
+    shapes = ((LAYERS, 2, COLS), (LAYERS, COLS), (LAYERS, 2, COLS), (LAYERS, 2, COLS), (LAYERS, 1024), (LAYERS, COLS))
+    return pl.pallas_call(
+        split_small,
+        out_shape=[jax.ShapeDtypeStruct((TOK, COLS), BF)] * 2 + [jax.ShapeDtypeStruct(d, F32) for d in shapes],
+        in_specs=[vmem] * 3,
+        out_specs=[vmem] * 8,
+        name="split_small",
+    )(hout, gin, sums)
+
+
 def shards(
     hidden_in, seg_ids, key_mask, w_qkv, qv_bias, w_out, out_bias, ln_gain, ln_shift,
     w_up, up_bias, w_down, down_bias, grad_out,
 ):
-    places = jnp.arange(TOK, dtype=jnp.int32)
-    allowed = (seg_ids[:, None] == seg_ids[None, :]) & (
-        (key_mask[None, :] == 1) | (places[:, None] == places[None, :])
+    hout, gin, grad_qkv, grad_out_w, grad_up, grad_down, sums = step_call(
+        hidden_in, grad_out, seg_ids.reshape(1, TOK), key_mask.reshape(1, TOK), out_bias, ln_gain, ln_shift, down_bias,
+        up_bias, qv_bias, w_qkv.transpose(0, 2, 1, 3), w_out, w_up, w_down,
     )
-    zero = jnp.zeros((LAYERS, COLS), F32)
-    small = jnp.stack(
-        [out_bias, ln_gain[:, 0], ln_shift[:, 0], ln_gain[:, 1], ln_shift[:, 1], down_bias, zero, zero], axis=1
-    ).reshape(LAYERS * 8, COLS)
-    hout, gin, big, sums = step_call(
-        hidden_in, grad_out, allowed.astype(F32), small, up_bias, qv_bias,
-        w_qkv.reshape(LAYERS, 512, 768), w_out, w_up, w_down,
-    )
-    big = big.astype(F32)
-    grad_down = big[:, 0:2].reshape(LAYERS, 1024, 512)
-    grad_up = jnp.concatenate([big[:, 2], big[:, 3]], axis=2)
-    value_part = jnp.concatenate([big[:, 5, 256:, :256], big[:, 5, 256:, 256:]], axis=1)
-    grad_qkv = jnp.concatenate([big[:, 4], value_part], axis=2).reshape(LAYERS, 512, 3, COLS)
-    grad_out_w = big[:, 5, :256]
-    feature = sums[:16].reshape(LAYERS, 8, COLS)
+    hout, gin, qvb, outb, gain, shift, upb, downb = split_call(hout, gin, sums)
     return (
         hout,
         gin,
-        grad_qkv,
-        sums[24:28].reshape(LAYERS, 2, COLS),
-        grad_out_w,
-        feature[:, 0],
-        jnp.stack([feature[:, 1], feature[:, 3]], axis=1),
-        jnp.stack([feature[:, 2], feature[:, 4]], axis=1),
-        grad_up,
-        sums[16:24].reshape(LAYERS, 1024),
-        grad_down,
-        feature[:, 5],
+        grad_qkv.astype(F32).transpose(0, 2, 1, 3),
+        qvb,
+        grad_out_w.astype(F32),
+        outb,
+        gain,
+        shift,
+        grad_up.astype(F32),
+        upb,
+        grad_down.astype(F32),
+        downb,
     )
 
 

time: 391 us -> 281 us (0.72)
  Pallas kernels: 358 us -> 271 us
  local copies, waits for them, and re-layouts: 24.2 us -> 0.01 us
    pallas_call x1, Pallas kernels: 358 us -> 269 us  [step_call(): pl.pallas_call(kernel, out_shape=[jax.ShapeDtypeStruct((TOK, COLS), BF),...]
    unnamed x12 -> x6, local copies, waits for them, and re-layouts: 7.78 us -> 0.01 us
    slice x5 -> x0, local copies, waits for them, and re-layouts: 6.52 us -> none  [the longest x1 4.34 us: shards(): grad_down = big[:, 0:2].reshape(LAYERS, 1024, 512)]
    convert_element_type x2 -> x3, other arithmetic: 3.29 us -> 7.93 us  [the longest x1 4.22 us: shards(): grad_up.astype(F32)]
where the time goes in v2:
time: 281 us
  Pallas kernels  271 us (96%)
  other arithmetic  9.88 us (4%)
    pallas_call x1, Pallas kernels, step_call(): pl.pallas_call(kernel, out_shape=[jax.ShapeDtypeStruct((TOK, COLS), BF),...  269 us

profile of v2, /device:TPU:0, one launch (start us, length us, event | category | flops | bytes accessed | tf_op | source)
XLA Modules:
  0.0 281.3 jit_solution(14087488276015068222)
XLA Ops:
  0.6 269.1 %encoder_step.1 = (bf16[256,256]{1,0:T(8,128)(2,1)}, bf16[256,256]{1,0:T(8,128)(2,1)}, bf16[2,3,512,256]{3,2,1,0:T(8,128)(2,1)}, bf16[2,256,512]{2,1,0:T(8,128)(...) custom-call(bf16[256,256]{1,0:T(8,128)(2,1)} %hid.1, ...), custom_call_target="tpu_custom_call" | custom-call | tf_op jit(solution)/shard_map/encoder_step/pallas_call | solution.py:779
  269.7 1.7 split_small.1
  271.4 0.0 copy-start
  271.4 4.2 %convert_element_type.11 = f32[2,512,1024]{2,1,0:T(8,128)} convert(bf16[2,512,1024]{2,1,0:T(8,128)(2,1)} %get-tuple-element.38) | non-fusion elementwise | flops 1048576 | bytes 6291456 | tf_op jit(solution)/shard_map/convert_element_type | solution.py:844
  275.6 0.0 copy-done
  275.6 0.0 copy-start.1
  275.6 2.6 convert_element_type.12
  278.2 0.0 copy-done.1
  278.2 0.0 copy-start.2
  278.3 1.9 convert_bitcast_fusion
  280.2 0.0 copy-done.2
  280.2 1.1 convert_element_type.10
Async XLA Ops:
  271.4 4.2 %copy-start = (bf16[2,1024,512]{2,1,0:T(8,128)(2,1)S(1)}, bf16[2,1024,512]{2,1,0:T(8,128)(2,1)}, u32[]{:S(2)}) copy-start(bf16[2,1024,512]{2,1,0:T(8,128)(2,1)} %get-tuple-element.40) | copy-start | bytes 6291460
  275.6 2.6 copy-start.1
  278.2 2.0 copy-start.2

commit v3 on v2

v3 whole, which is shorter than its diff:
```python
import functools

import jax
import jax.numpy as jnp
from jax import lax
from jax.experimental import pallas as pl
from jax.experimental.pallas import tpu as pltpu
from jax.sharding import PartitionSpec as P

D = 1024
HD = 64
LAYERS = 2
TOK = 256
OWN = 64
COLS = 256
HEADS_LOCAL = 4
SLABS = 6
EPSILON = 1e-05
MASKED = -1e30
SCALE = HD**-0.5
PARTS = ((0, 1, 2, 0), (0, 2, 3, 1), (1, 0, 512, 0), (2, 0, 512, 0), (2, 512, 1024, 1), (3, 0, 256, 0), (3, 256, 512, 1))
WEIGHT_ROWS = (512, 256, 512, 1024)
MESH = pl.DeviceIdType.MESH
BF = jnp.bfloat16
F32 = jnp.float32


def dot(a, b):
    return jnp.dot(a, b, preferred_element_type=F32)


def dot_nt(a, b):
    return lax.dot_general(a, b, (((1,), (1,)), ((), ())), preferred_element_type=F32)


def dot_tn(a, b):
    return lax.dot_general(a, b, (((0,), (0,)), ((), ())), preferred_element_type=F32)


def norm_back(upstream, normed, inverse, gain):
    scaled = upstream * gain
    mean_one = jnp.sum(scaled, axis=1, keepdims=True) / D
    mean_two = jnp.sum(scaled * normed, axis=1, keepdims=True) / D
    return inverse * (scaled - mean_one - normed * mean_two)


def kernel(
    hid, gout, seg, key, outb, gain, shift, downb, upb, qvb, wq, wo, wu, wd,
    hout, gin, gq, go, gu, gd, gsmall,
    mask, small, WQ, WO, WU, WD, PF, A2H, A2G, S, M, U, GS, GF, F1,
    STATE, MID, SEC, FIR, QKV, CTX, PR, DG, ACT, NRM, INV, LL, ML, GC,
    PS, XS, L1, L2, HS, HOB, GIB,
    G, RL, R1, A1, R2, A2, R3, FB,
    SGF, SU, SQ, RC, SM, SZ, SY, SR,
    w_s, w_r, w_rb, wd_s, wd_r, w_lsem, in_s, in_r, ag_s, ag_r, rs_s, rs_r, gr_s, gr_r, out_s, out_r, lsem, sm_s, sm_r,
):
    dp = lax.axis_index("dp")
    row = lax.axis_index("row")
    col = lax.axis_index("col")
    z, y = lax.div(dp, 4), lax.rem(dp, 4)
    xh, core = lax.div(col, 2), lax.rem(col, 2)
    col_core = xh * 2 + (1 - core)
    col_cross = (1 - xh) * 2 + core
    col_diag = (1 - xh) * 2 + (1 - core)
    core_dev = (dp, row, col_core)
    cross_dev = (dp, row, col_cross)
    row_dev = (dp, 1 - row, col)

    def col_dev(d):
        return (dp, row, lax.rem(col + d, 4))

    def axis_place(axis):
        return z if axis == 0 else y

    def axis_dev(axis, d):
        if axis == 0:
            return (lax.rem(z + d, 4) * 4 + y, row, col)
        return (z * 4 + lax.rem(y + d, 4), row, col)

    def chunk(j, rows=OWN):
        return pl.ds(pl.multiple_of(j * rows, rows), rows)

    def remote(src, dst, ssem, rsem, dev):
        return pltpu.make_async_remote_copy(
            src_ref=src, dst_ref=dst, send_sem=ssem, recv_sem=rsem, device_id=dev, device_id_type=MESH
        )

    def arrived(ref, sem):
        pltpu.make_async_copy(ref, ref, sem).wait()

    barrier = pltpu.get_barrier_semaphore()
    for dev in [col_dev(1), col_dev(2), col_dev(3), row_dev] + [axis_dev(a, d) for a in (0, 1) for d in (1, 2, 3)]:
        pl.semaphore_signal(barrier, 1, device_id=dev, device_id_type=MESH)
    pl.semaphore_wait(barrier, 10)

    def in_copies(d):
        to = lax.rem(col + d, 4)
        dev = (dp, row, to)
        return [
            remote(hid.at[chunk(to)], A2H.at[:, chunk(col, COLS)], in_s.at[0], in_r.at[0], dev),
            remote(small, PF.at[:, chunk(col, COLS)], in_s.at[1], in_r.at[1], dev),
            remote(gout.at[chunk(to)], A2G.at[:, chunk(col, COLS)], in_s.at[2], in_r.at[2], dev),
        ]

    for l in range(LAYERS):
        rows = (outb[l : l + 1], gain[l, 0:1], shift[l, 0:1], gain[l, 1:2], shift[l, 1:2], downb[l : l + 1])
        for r in range(6):
            small[l * 8 + r : l * 8 + r + 1, :] = rows[r]
        small[l * 8 + 6 : l * 8 + 8, :] = jnp.zeros((2, COLS), F32)
    for d in (1, 2, 3):
        for c in in_copies(d)[:2]:
            c.start()

    pairs = ((wq, WQ), (wo, WO), (wu, WU), (wd, WD))

    def region(ref, n, lo, hi, rows):
        if n == 0:
            return ref.at[lo, rows, :]
        return ref.at[rows, pl.ds(lo, hi - lo)]

    def w_local(l, n):
        return pltpu.make_async_copy(pairs[n][0].at[l], pairs[n][1].at[l, row], w_lsem.at[l, n])

    def w_direct(l, which):
        return remote(wq.at[l, 0], WQ.at[l, which, 0], wd_s.at[l], wd_r.at[l], row_dev)

    def part_axes(p):
        first = PARTS[p][3]
        return first, 1 - first

    def part_rows(p, a_place, b_place):
        piece = WEIGHT_ROWS[PARTS[p][0]] // 16
        return pl.ds(pl.multiple_of((b_place * 4 + a_place) * piece, piece), piece)

    def w_piece(l, p, which):
        n, lo, hi, _ = PARTS[p]
        first, second = part_axes(p)
        rows = part_rows(p, axis_place(first), axis_place(second))
        return remote(
            region(pairs[n][0].at[l], n, lo, hi, rows), region(pairs[n][1].at[l, which], n, lo, hi, rows),
            w_s.at[l, 0], w_r.at[l, p, 0], row_dev,
        )

    def w_one(l, p, d, place):
        n, lo, hi, _ = PARTS[p]
        first, second = part_axes(p)
        rows = part_rows(p, place, axis_place(second))
        ref = region(pairs[n][1].at[l, 1 - row], n, lo, hi, rows)
        return remote(ref, ref, w_s.at[l, 1], w_r.at[l, p, 1], axis_dev(first, d))

    def w_two(l, p, d, place):
        n, lo, hi, _ = PARTS[p]
        _, second = part_axes(p)
        block = WEIGHT_ROWS[n] // 4
        ref = region(pairs[n][1].at[l, 1 - row], n, lo, hi, chunk(place, block))
        return remote(ref, ref, w_s.at[l, 2], w_rb.at[l, n], axis_dev(second, d))

    def w_step_one(l, p):
        w_piece(l, p, 1 - row).wait_recv()
        for d in (1, 2, 3):
            w_one(l, p, d, axis_place(part_axes(p)[0])).start()

    def three_pieces(l, p):
        n, lo, hi, _ = PARTS[p]
        piece = WEIGHT_ROWS[n] // 16
        return region(pairs[n][1].at[l, 1 - row], n, lo, hi, pl.ds(0, 3 * piece))

    def w_step_two(l, p):
        second = part_axes(p)[1]
        arrived(three_pieces(l, p), w_r.at[l, p, 1])
        for d in (1, 2, 3):
            w_two(l, p, d, axis_place(second)).start()

    def w_wait(l, n):
        w_local(l, n).wait()
        rows = WEIGHT_ROWS[n] * 3 // 4
        if n == 0:
            w_direct(l, 1 - row).wait_recv()
            arrived(WQ.at[l, 1 - row, pl.ds(0, 2), pl.ds(0, rows), :], w_rb.at[l, n])
        else:
            arrived(pairs[n][1].at[l, 1 - row, pl.ds(0, rows), :], w_rb.at[l, n])

    def w_drain(l):
        w_direct(l, row).wait_send()
        arrived(WU.at[0, 0, pl.ds(0, 176), pl.ds(0, 512)], w_s.at[l, 0])
        arrived(WQ.at[0, :, :, pl.ds(0, 176), :], w_s.at[l, 1])
        arrived(WQ.at[:, :, :, pl.ds(0, 352), :], w_s.at[l, 2])

    parts = range(len(PARTS))
    for p in parts:
        w_piece(0, p, row).start()
    w_direct(0, row).start()
    for n in range(4):
        w_local(0, n).start()
    for p in parts:
        w_step_one(0, p)
    for d in (1, 2, 3):
        in_copies(d)[2].start()
    for n in range(4):
        w_local(1, n).start()

    seg_lanes = jnp.broadcast_to(seg[...].astype(F32), (TOK, TOK))
    key_lanes = jnp.broadcast_to(key[...].astype(F32), (TOK, TOK))
    same_place = lax.broadcasted_iota(jnp.int32, (TOK, TOK), 0) == lax.broadcasted_iota(jnp.int32, (TOK, TOK), 1)
    keep = jnp.where(same_place, 1.0, key_lanes)
    mask[...] = jnp.where(seg_lanes.T == seg_lanes, keep, 0.0)

    A2H[:, chunk(col, COLS)] = hid[chunk(col), :]
    A2G[:, chunk(col, COLS)] = gout[chunk(col), :]
    PF[:, chunk(col, COLS)] = small[...]
    arrived(A2H.at[:, pl.ds(0, 3 * COLS)], in_r.at[0])
    arrived(PF.at[:, pl.ds(0, 3 * COLS)], in_r.at[1])
    arrived(A2G.at[:, pl.ds(0, 3 * COLS)], in_r.at[2])
    S[...] = A2H[...].astype(F32)
    U[...] = A2G[...].astype(F32)
    w_step_two(0, 0)
    w_step_two(0, 1)

    def ag_rows(owner, p):
        return pl.ds(pl.multiple_of(owner * OWN + p * 32, 32), 32)

    def ag_send(X):
        out = []
        for p in (0, 1):
            rows = ag_rows(col, p)
            out.append(remote(X.at[rows], X.at[rows], ag_s.at[0], ag_r.at[p], cross_dev))
        out.append(remote(X.at[chunk(col)], X.at[chunk(col)], ag_s.at[0], ag_r.at[2], core_dev))
        return out

    def ag_start(X):
        for c in ag_send(X):
            c.start()

    def ag_finish(X):
        for p in (0, 1):
            rows = ag_rows(col_cross, p)
            arrived(X.at[rows], ag_r.at[p])
            remote(X.at[rows], X.at[rows], ag_s.at[0], ag_r.at[3], core_dev).start()
        arrived(X.at[chunk(col_core)], ag_r.at[2])
        arrived(X.at[chunk(col_diag)], ag_r.at[3])

    def ag_drain(X):
        arrived(X.at[pl.ds(0, 3 * OWN)], ag_s.at[0])

    def half(h):
        return pl.ds(h * 512, 512)

    def rs_first(par, h, t):
        to = (1 - xh) * 2 + (1 - core) if t == 0 else col_core
        return remote(
            PS.at[chunk(to), half(h)], L1.at[par, t, :, half(h)], rs_s.at[0], rs_r.at[h * 3 + t], core_dev
        )

    def rs_cross(par, h):
        return remote(XS.at[:, half(h)], L2.at[par, :, half(h)], rs_s.at[0], rs_r.at[h * 3 + 2], cross_dev)

    def rs_send(par, h):
        for t in (0, 1):
            rs_first(par, h, t).start()

    def rs_mid(par, h):
        rs_first(par, h, 0).wait_recv()
        total = PS[chunk(col_cross), half(h)].astype(F32) + L1[par, 0, :, half(h)].astype(F32)
        XS[:, half(h)] = total.astype(BF)
        rs_cross(par, h).start()

    def rs_end(par, h):
        rs_first(par, h, 1).wait_recv()
        total = PS[chunk(col), half(h)].astype(F32) + L1[par, 1, :, half(h)].astype(F32)
        rs_cross(par, h).wait_recv()
        return total + L2[par, :, half(h)].astype(F32)

    def rs_drain():
        arrived(PS.at[pl.ds(0, 3 * OWN)], rs_s.at[0])

    first_half, second_half = pl.ds(0, 256), pl.ds(256, 256)

    def gr_block(l, s, d, lanes):
        return G.at[l, s, :, chunk(lax.rem(axis_place(s % 2) + d, 4), 128), lanes]

    def gr_relay(l, s, side):
        lanes, d = ((first_half, 1), (second_half, 3))[side]
        return remote(gr_block(l, s, 2, lanes), RL.at[l, s, side], gr_s.at[l, 0], gr_r.at[l, s, 0], axis_dev(s % 2, d))

    def gr_one(l, s, side, lanes):
        d = (1, 3)[side]
        return remote(
            gr_block(l, s, d, lanes), R1.at[l, s, side, :, :, lanes], gr_s.at[l, 1], gr_r.at[l, s, 1], axis_dev(s % 2, d)
        )

    def gr_two(l, s, d):
        axis = 1 - s % 2
        to = lax.rem(axis_place(axis) + d, 4)
        return remote(A1.at[l, s, :, chunk(to, 32), :], R2.at[l, s, d - 1], gr_s.at[l, 2], gr_r.at[l, s, 2], axis_dev(axis, d))

    def gr_row(l, s):
        return remote(A2.at[l, s, 1 - row], R3.at[l, s], gr_s.at[l, 3], gr_r.at[l, s, 3], row_dev)

    def gr_four(l, s, d, place):
        rows = FB.at[l, s, chunk(place, 32), :]
        return remote(rows, rows, gr_s.at[l, 4], gr_r.at[l, s, 4], axis_dev(1 - s % 2, d))

    def places(l, s, place):
        every = pl.ds(0, 512)
        if s < 4:
            out = []
            for q in (0, 1):
                if s < 2:
                    to = gd.at[l, pl.ds(pl.multiple_of(s * 512 + place * 128 + q * 64, 64), 64), :]
                else:
                    to = gu.at[l, pl.ds(pl.multiple_of(place * 128 + q * 64, 64), 64), pl.ds((s - 2) * 512, 512)]
                out.append([(pl.ds(q * 64, 64), every, to)])
            return out
        if s == 4:
            return [[(pl.ds(0, 128), pl.ds(j * COLS, COLS), gq.at[l, j, chunk(place, 128), :])] for j in (0, 1)]
        lower = pl.ds(64, 64)
        return [
            [(pl.ds(0, 64), every, go.at[l, chunk(place, 64), :])],
            [
                (lower, pl.ds(0, COLS), gq.at[l, 2, chunk(place, 64), :]),
                (lower, pl.ds(COLS, COLS), gq.at[l, 2, pl.ds(pl.multiple_of(256 + place * 64, 64), 64), :]),
            ],
        ]

    def gr_five(l, s, d):
        first, second = places(l, s, axis_place(s % 2))
        return [
            remote(FB.at[l, s, rows, lanes], to, gr_s.at[l, 5], gr_r.at[l, s, 5], axis_dev(s % 2, d))
            for rows, lanes, to in first + second
        ]

    def gr_six(l, s):
        out = []
        for side, (source, d) in enumerate(((3, 1), (1, 3))):
            place = lax.rem(axis_place(s % 2) + source, 4)
            for _, _, to in places(l, s, place)[side]:
                out.append(remote(to, to, gr_s.at[l, 6], gr_r.at[l, s, 6], axis_dev(s % 2, d)))
        return out

    def gr_local(l, s):
        first, second = places(l, s, axis_place(s % 2))
        return [pltpu.make_async_copy(FB.at[l, s, rows, lanes], to, lsem.at[l]) for rows, lanes, to in first + second]

    def t1(l, s):
        gr_relay(l, s, 0).start()
        gr_relay(l, s, 1).start()
        gr_one(l, s, 0, second_half).start()
        gr_one(l, s, 1, first_half).start()

    def t1b(l, s):
        arrived(RL.at[l, s], gr_r.at[l, s, 0])
        for side, lanes in ((0, first_half), (1, second_half)):
            rows = chunk(lax.rem(axis_place(s % 2) + (1, 3)[side], 4), 128)
            for r in (0, 1):
                total = G[l, s, r, rows, lanes].astype(F32) + RL[l, s, side, r].astype(F32)
                G[l, s, r, rows, lanes] = total.astype(BF)
            gr_one(l, s, side, lanes).start()

    def t2(l, s):
        arrived(R1.at[l, s], gr_r.at[l, s, 1])
        own = chunk(axis_place(s % 2), 128)
        for r in (0, 1):
            total = G[l, s, r, own, :].astype(F32)
            for side in (0, 1):
                total = total + R1[l, s, side, r].astype(F32)
            A1[l, s, r] = total.astype(BF)
        for d in (1, 2, 3):
            gr_two(l, s, d).start()

    def t3(l, s):
        arrived(R2.at[l, s], gr_r.at[l, s, 2])
        own = chunk(axis_place(1 - s % 2), 32)
        for r in (0, 1):
            total = A1[l, s, r, own, :].astype(F32)
            for d in (0, 1, 2):
                total = total + R2[l, s, d, r].astype(F32)
            A2[l, s, r] = total.astype(BF)
        gr_row(l, s).start()

    def t4(l, s):
        arrived(R3.at[l, s], gr_r.at[l, s, 3])
        place = axis_place(1 - s % 2)
        FB[l, s, chunk(place, 32), :] = (A2[l, s, row].astype(F32) + R3[l, s].astype(F32)).astype(BF)
        for d in (1, 2, 3):
            gr_four(l, s, d, place).start()

    def t5(l, s):
        arrived(FB.at[l, s, pl.ds(0, 96), :], gr_r.at[l, s, 4])
        for d in (1, 3):
            for c in gr_five(l, s, d):
                c.start()
        for c in gr_local(l, s):
            c.start()

    def t5b(l, s):
        arrived(R1.at[l, s, 0], gr_r.at[l, s, 5])
        for c in gr_six(l, s):
            c.start()

    def t6(l, s):
        arrived(FB.at[l, s], gr_r.at[l, s, 6])

    def gr_drain(l):
        arrived(FB.at[l], lsem.at[l])
        arrived(RL.at[l], gr_s.at[l, 0])
        arrived(R1.at[l], gr_s.at[l, 1])
        arrived(R2.at[l], gr_s.at[l, 2])
        arrived(R3.at[l], gr_s.at[l, 3])
        arrived(FB.at[l, :, pl.ds(0, 96), :], gr_s.at[l, 4])
        arrived(R1.at[l, :, 0], gr_s.at[l, 5])
        arrived(FB.at[l], gr_s.at[l, 6])

    def both(step, l, first):
        step(l, first)
        step(l, first + 1)

    def vec(l, r):
        return PF[pl.ds(l * 8 + r, 1), :]

    def norm_into(values, l, n, gain, shift):
        mean_row = jnp.sum(values, axis=1, keepdims=True) / D
        squares = jnp.sum(values * values, axis=1, keepdims=True) / D
        inverse = lax.rsqrt(squares - mean_row * mean_row + EPSILON)
        normed = (values - mean_row) * inverse
        NRM[l, n] = normed
        INV[l, n] = jnp.broadcast_to(inverse, (OWN, 128))
        return normed * gain + shift

    def forward(l, carry):
        X = STATE.at[l]
        X[chunk(col), :] = S[...].astype(BF)
        ag_start(X)

        @pl.when(l == 0)
        def _():
            for p in parts[2:]:
                w_step_two(0, p)
            for p in parts:
                w_piece(1, p, row).start()
            w_direct(1, row).start()

        w_wait(l, 0)
        ag_finish(X)
        for j in range(3):
            mixed = dot(STATE[l, :, :512], WQ[l, 0, j]) + dot(STATE[l, :, 512:], WQ[l, 1, j])
            if j != 1:
                mixed = mixed + qvb[l, j // 2 : j // 2 + 1, :]
            QKV[l, j] = mixed.astype(BF)
        ag_drain(X)

        @pl.when(l == 0)
        def _():
            for p in parts:
                w_step_one(1, p)

        for h in range(HEADS_LOCAL):
            lanes = slice(h * HD, (h + 1) * HD)
            scores = dot_nt(QKV[l, 0, :, lanes], QKV[l, 1, :, lanes])
            scaled = jnp.where(mask[...] > 0.5, scores * SCALE, MASKED)
            raised = jnp.exp(scaled - jnp.max(scaled, axis=1, keepdims=True))
            probs = raised / jnp.sum(raised, axis=1, keepdims=True)
            PR[l, h] = probs
            CTX[l, :, lanes] = dot(probs.astype(BF), QKV[l, 2, :, lanes]).astype(BF)

        @pl.when(l == 0)
        def _():
            for p in parts:
                w_step_two(1, p)

        w_wait(l, 1)
        for h in (0, 1):
            PS[:, half(h)] = dot(CTX[l], WO[l, h]).astype(BF)
            rs_send(0, h)
        rs_mid(0, 0)
        rs_mid(0, 1)
        for h in (0, 1):
            F1[:, half(h)] = S[:, half(h)] + rs_end(0, h)
        rs_drain()
        middle = norm_into(F1[...] + vec(l, 0), l, 0, vec(l, 1), vec(l, 2))
        M[...] = middle
        X = MID.at[l]
        X[chunk(col), :] = middle.astype(BF)
        ag_start(X)
        w_wait(l, 2)
        ag_finish(X)

        def lift(n, c):
            lanes = chunk(n, COLS)
            lifted = dot(MID[l, :, :512], WU[l, 0, :, lanes]) + dot(MID[l, :, 512:], WU[l, 1, :, lanes])
            lifted = lifted + upb[pl.ds(l, 1), lanes]
            phi = 0.5 * (1.0 + lax.erf(lifted * (0.5**0.5)))
            density = jnp.exp(-0.5 * lifted * lifted) * 0.3989422804014327
            DG[l, :, lanes] = phi + lifted * density
            ACT[l, :, lanes] = (lifted * phi).astype(BF)
            return c

        lax.fori_loop(0, 4, lift, 0)
        ag_drain(X)
        w_wait(l, 3)
        for h in (0, 1):
            for q in (0, 1):
                lanes = pl.ds(h * 512 + q * 256, 256)
                PS[:, lanes] = dot(ACT[l], WD[l, h, :, pl.ds(q * 256, 256)]).astype(BF)
            rs_send(1, h)
        rs_mid(1, 0)
        rs_mid(1, 1)
        for h in (0, 1):
            F1[:, half(h)] = M[:, half(h)] + rs_end(1, h)
        rs_drain()
        S[...] = norm_into(F1[...] + vec(l, 5), l, 1, vec(l, 3), vec(l, 4))
        return carry

    lax.fori_loop(0, LAYERS, forward, 0)

    def out_copies(n, d):
        buf = (HOB, GIB)[n]
        to = lax.rem(col + d, 4)
        return remote(
            HS.at[n, :, chunk(to, COLS)], buf.at[chunk(col)], out_s.at[n], out_r.at[n], (dp, row, to)
        )

    HS[0] = S[...].astype(BF)
    for d in (1, 2, 3):
        out_copies(0, d).start()
    HOB[chunk(col), :] = HS[0, :, chunk(col, COLS)]

    def backward(i, carry):
        l = LAYERS - 1 - i
        prev = l + 1
        upstream = U[...]
        normed = NRM[l, 1]
        SGF[l, 3:4, :] = jnp.sum(upstream * normed, axis=0, keepdims=True)
        SGF[l, 4:5, :] = jnp.sum(upstream, axis=0, keepdims=True)
        grad_second = norm_back(upstream, normed, INV[l, 1, :, :1], vec(l, 3))
        GS[...] = grad_second
        SGF[l, 5:6, :] = jnp.sum(grad_second, axis=0, keepdims=True)
        SEC[chunk(col), :] = grad_second.astype(BF)
        ag_start(SEC)

        @pl.when(i > 0)
        def _():
            both(t2, prev, 2)
            both(t3, prev, 0)
            both(t1b, prev, 4)

        ag_finish(SEC)

        def pull(n, c):
            lanes = chunk(n, COLS)
            grad_act = dot_nt(SEC[:, :512], WD[l, 0, lanes, :]) + dot_nt(SEC[:, 512:], WD[l, 1, lanes, :])
            grad_lifted = grad_act * DG[l, :, lanes]
            SU[l, :, lanes] = jnp.sum(grad_lifted, axis=0, keepdims=True)
            LL[:, lanes] = grad_lifted.astype(BF)
            return c

        lax.fori_loop(0, 4, pull, 0)
        for h in (0, 1):
            for q in (0, 1):
                lanes = pl.ds(h * 512 + q * 256, 256)
                PS[:, lanes] = dot_nt(LL[...], WU[l, h, pl.ds(q * 256, 256), :]).astype(BF)
            rs_send(0, h)
        rs_mid(0, 0)
        rs_mid(0, 1)

        def down_grad(f, c):
            total = dot_tn(ACT[l, :, chunk(f, COLS)], SEC[...]).astype(BF)
            rows = chunk(lax.rem(f, 2), COLS)
            for r in (0, 1):
                G[l, lax.div(f, 2), r, rows, :] = total[:, r * 512 : (r + 1) * 512]
            return c

        lax.fori_loop(0, 4, down_grad, 0)
        both(t1, l, 0)
        ag_drain(SEC)

        @pl.when(i > 0)
        def _():
            both(t4, prev, 0)
            both(t3, prev, 2)
            both(t2, prev, 4)

        for h in (0, 1):
            GS[:, half(h)] = GS[:, half(h)] + rs_end(0, h)
        rs_drain()
        grad_middle = GS[...]
        normed = NRM[l, 0]
        SGF[l, 1:2, :] = jnp.sum(grad_middle * normed, axis=0, keepdims=True)
        SGF[l, 2:3, :] = jnp.sum(grad_middle, axis=0, keepdims=True)
        grad_first = norm_back(grad_middle, normed, INV[l, 0, :, :1], vec(l, 1))
        GF[...] = grad_first
        SGF[l, 0:1, :] = jnp.sum(grad_first, axis=0, keepdims=True)
        FIR[chunk(col), :] = grad_first.astype(BF)
        ag_start(FIR)

        def up_grad(n, c):
            total = dot_tn(MID[l, :, chunk(n, COLS)], LL[...]).astype(BF)
            rows = chunk(lax.rem(n, 2), COLS)
            for r in (0, 1):
                G[l, 2 + r, lax.div(n, 2), rows, :] = total[:, r * 512 : (r + 1) * 512]
            return c

        lax.fori_loop(0, 4, up_grad, 0)
        both(t1, l, 2)

        @pl.when(i > 0)
        def _():
            both(t5, prev, 0)
            both(t4, prev, 2)
            both(t3, prev, 4)

        both(t1b, l, 0)

        ag_finish(FIR)
        GC[...] = (dot_nt(FIR[:, :512], WO[l, 0]) + dot_nt(FIR[:, 512:], WO[l, 1])).astype(BF)
        for h in range(HEADS_LOCAL):
            lanes = slice(h * HD, (h + 1) * HD)
            probs = PR[l, h]
            grad_probs = dot_nt(GC[:, lanes], QKV[l, 2, :, lanes])
            centre = jnp.sum(probs * grad_probs, axis=1, keepdims=True)
            grad_scores = (probs * (grad_probs - centre) * SCALE).astype(BF)
            grad_query = dot(grad_scores, QKV[l, 1, :, lanes])
            grad_key = dot_tn(grad_scores, QKV[l, 0, :, lanes])
            grad_value = dot_tn(probs.astype(BF), GC[:, lanes])
            SQ[l, 0:1, lanes] = jnp.sum(grad_query, axis=0, keepdims=True)
            SQ[l, 1:2, lanes] = jnp.sum(grad_value, axis=0, keepdims=True)
            ML[:, h * HD : (h + 1) * HD] = grad_query.astype(BF)
            ML[:, COLS + h * HD : COLS + (h + 1) * HD] = grad_key.astype(BF)
            ML[:, 2 * COLS + h * HD : 2 * COLS + (h + 1) * HD] = grad_value.astype(BF)
        for h in (0, 1):
            for q in (0, 1):
                lanes = pl.ds(h * 512 + q * 256, 256)
                PS[:, lanes] = sum(
                    dot_nt(ML[:, j * COLS : (j + 1) * COLS], WQ[l, h, j, pl.ds(q * 256, 256), :]) for j in range(3)
                ).astype(BF)
            rs_send(1, h)
        rs_mid(1, 0)
        rs_mid(1, 1)
        total = dot_tn(CTX[l], FIR[...]).astype(BF)
        for r in (0, 1):
            for q in range(4):
                G[l, 5, r, q * 128 : q * 128 + 64, :] = total[q * 64 : (q + 1) * 64, r * 512 : (r + 1) * 512]

        def qkv_grad(r, c):
            for q in (0, 1):
                total = dot_tn(STATE[l, :, chunk(2 * r + q, COLS)], ML[...]).astype(BF)
                G[l, 4, r, q * 256 : (q + 1) * 256, :] = total[:, :512]
                for b in range(4):
                    G[l, 5, r, b * 128 + 64 : b * 128 + 128, q * 256 : (q + 1) * 256] = total[b * 64 : (b + 1) * 64, 512:]
            return c

        lax.fori_loop(0, 2, qkv_grad, 0)
        both(t1, l, 4)
        ag_drain(FIR)
        both(t1b, l, 2)
        both(t2, l, 0)

        @pl.when(i > 0)
        def _():
            both(t5, prev, 2)
            both(t4, prev, 4)
            both(t5b, prev, 0)

        for h in (0, 1):
            U[:, half(h)] = GF[:, half(h)] + rs_end(1, h)
        rs_drain()
        return carry

    lax.fori_loop(0, LAYERS, backward, 0)

    HS[1] = U[...].astype(BF)
    for d in (1, 2, 3):
        out_copies(1, d).start()
    GIB[chunk(col), :] = HS[1, :, chunk(col, COLS)]

    def sc_copy(d):
        to = lax.rem(col + d, 4)
        return remote(SGF.at[:, :, chunk(to, COLS)], RC.at[d - 1], sm_s.at[0], sm_r.at[0], (dp, row, to))

    def sd_copy(axis, d, place):
        buf = (SZ, SY)[axis]
        return remote(
            buf.at[axis_place(axis)], buf.at[place], sm_s.at[1 + axis], sm_r.at[1 + axis], axis_dev(axis, d)
        )

    def sr_copy():
        return remote(SM, SR, sm_s.at[3], sm_r.at[3], row_dev)

    for d in (1, 2, 3):
        sc_copy(d).start()
    both(t2, 0, 2)
    both(t5b, 1, 2)
    both(t5, 1, 4)
    both(t3, 0, 0)
    both(t1b, 0, 4)
    arrived(RC, sm_r.at[0])
    feature = SGF[:, :, chunk(col, COLS)]
    for d in (0, 1, 2):
        feature = feature + RC[d]
    for l in range(LAYERS):
        SZ[z, 8 * l : 8 * l + 8, :] = feature[l]
        for q in range(4):
            SZ[z, 16 + 4 * l + q : 17 + 4 * l + q, :] = SU[l, :, q * COLS : (q + 1) * COLS]
        SZ[z, 24 + 2 * l : 26 + 2 * l, :] = SQ[l]
    SZ[z, 28:32, :] = jnp.zeros((4, COLS), F32)
    for d in (1, 2, 3):
        sd_copy(0, d, z).start()
    both(t4, 0, 0)
    both(t3, 0, 2)
    both(t2, 0, 4)
    both(t5b, 1, 4)
    arrived(SZ.at[pl.ds(0, 3)], sm_r.at[1])
    SY[y] = SZ[0] + SZ[1] + SZ[2] + SZ[3]
    for d in (1, 2, 3):
        sd_copy(1, d, y).start()
    both(t5, 0, 0)
    both(t4, 0, 2)
    both(t3, 0, 4)
    arrived(SY.at[pl.ds(0, 3)], sm_r.at[2])
    SM[...] = SY[0] + SY[1] + SY[2] + SY[3]
    sr_copy().start()
    both(t5b, 0, 0)
    both(t5, 0, 2)
    both(t4, 0, 4)
    sr_copy().wait_recv()
    gsmall[...] = SM[...] + SR[...]
    both(t5b, 0, 2)
    both(t5, 0, 4)
    for n in (0, 1):
        buf = (HOB, GIB)[n]
        arrived(buf.at[pl.ds(0, 3 * OWN)], out_r.at[n])
    hout[...] = HOB[...]
    gin[...] = GIB[...]
    both(t5b, 0, 4)

    arrived(A2H.at[:, pl.ds(0, 3 * COLS)], in_s.at[0])
    arrived(PF.at[:, pl.ds(0, 3 * COLS)], in_s.at[1])
    arrived(A2G.at[:, pl.ds(0, 3 * COLS)], in_s.at[2])
    for n in (0, 1):
        arrived(HOB.at[pl.ds(0, 3 * OWN)], out_s.at[n])
    arrived(RC, sm_s.at[0])
    arrived(SZ.at[pl.ds(0, 3)], sm_s.at[1])
    arrived(SY.at[pl.ds(0, 3)], sm_s.at[2])
    sr_copy().wait_send()

    def finish(l, c):
        w_drain(l)
        for s in range(SLABS):
            t6(l, s)
        gr_drain(l)
        return c

    lax.fori_loop(0, LAYERS, finish, 0)


def step_call(*args):
    vmem = pl.BlockSpec(memory_space=pltpu.VMEM)
    hbm = pl.BlockSpec(memory_space=pl.ANY)
    dma = pltpu.SemaphoreType.DMA
    V = pltpu.VMEM
    L = LAYERS
    scratch = [
        V((TOK, TOK), F32), V((16, COLS), F32),
        V((L, 2, 3, 512, COLS), BF), V((L, 2, 256, 512), BF), V((L, 2, 512, 1024), BF), V((L, 2, 1024, 512), BF),
        V((16, 1024), F32), V((OWN, D), BF), V((OWN, D), BF),
        V((OWN, D), F32), V((OWN, D), F32), V((OWN, D), F32), V((OWN, D), F32), V((OWN, D), F32), V((OWN, D), F32),
        V((L, TOK, D), BF), V((L, TOK, D), BF), V((TOK, D), BF), V((TOK, D), BF),
        V((L, 3, TOK, COLS), BF), V((L, TOK, COLS), BF), V((L, HEADS_LOCAL, TOK, TOK), F32),
        V((L, TOK, 1024), F32), V((L, TOK, 1024), BF), V((L, 2, OWN, D), F32), V((L, 2, OWN, 128), F32),
        V((TOK, 1024), BF), V((TOK, 768), BF), V((TOK, COLS), BF),
        V((TOK, D), BF), V((OWN, D), BF), V((2, 2, OWN, D), BF), V((2, OWN, D), BF),
        V((2, OWN, D), BF), V((TOK, COLS), BF), V((TOK, COLS), BF),
        V((L, SLABS, 2, 512, 512), BF), V((L, SLABS, 2, 2, 128, 256), BF),
        V((L, SLABS, 2, 2, 128, 512), BF), V((L, SLABS, 2, 128, 512), BF),
        V((L, SLABS, 3, 2, 32, 512), BF), V((L, SLABS, 2, 32, 512), BF), V((L, SLABS, 32, 512), BF),
        V((L, SLABS, 128, 512), BF),
        V((L, 8, D), F32), V((L, 1, 1024), F32), V((L, 2, COLS), F32), V((3, L, 8, COLS), F32),
        V((32, COLS), F32), V((4, 32, COLS), F32), V((4, 32, COLS), F32), V((32, COLS), F32),
        dma((L, 3)), dma((L, 7, 2)), dma((L, 4)), dma((L,)), dma((L,)), dma((L, 4)), dma((3,)), dma((3,)),
        dma((1,)), dma((4,)), dma((1,)), dma((6,)),
        dma((L, 7)), dma((L, SLABS, 7)), dma((2,)), dma((2,)), dma((L,)), dma((4,)), dma((4,)),
    ]
    return pl.pallas_call(
        kernel,
        out_shape=[
            jax.ShapeDtypeStruct((TOK, COLS), BF),
            jax.ShapeDtypeStruct((TOK, COLS), BF),
            jax.ShapeDtypeStruct((L, 3, 512, COLS), BF),
            jax.ShapeDtypeStruct((L, 256, 512), BF),
            jax.ShapeDtypeStruct((L, 512, 1024), BF),
            jax.ShapeDtypeStruct((L, 1024, 512), BF),
            jax.ShapeDtypeStruct((32, COLS), F32),
        ],
        in_specs=[vmem] * 10 + [hbm] * 4,
        out_specs=[vmem, vmem, hbm, hbm, hbm, hbm, vmem],
        scratch_shapes=scratch,
        compiler_params=pltpu.CompilerParams(
            collective_id=0, has_side_effects=True, vmem_limit_bytes=63 * 2**20
        ),
        name="encoder_step",
    )(*args)


def split_small(hout, gin, sums, out_h, out_g, qvb, outb, gain, shift, upb, downb):
    out_h[...] = hout[...]
    out_g[...] = gin[...]
    for l in range(LAYERS):
        outb[l : l + 1, :] = sums[8 * l : 8 * l + 1, :]
        for n in (0, 1):
            gain[l, n : n + 1, :] = sums[8 * l + 1 + 2 * n : 8 * l + 2 + 2 * n, :]
            shift[l, n : n + 1, :] = sums[8 * l + 2 + 2 * n : 8 * l + 3 + 2 * n, :]
        downb[l : l + 1, :] = sums[8 * l + 5 : 8 * l + 6, :]
        for q in range(4):
            upb[l : l + 1, q * COLS : (q + 1) * COLS] = sums[16 + 4 * l + q : 17 + 4 * l + q, :]
        qvb[l] = sums[24 + 2 * l : 26 + 2 * l, :]


def split_call(hout, gin, sums):
    vmem = pl.BlockSpec(memory_space=pltpu.VMEM)
    shapes = ((LAYERS, 2, COLS), (LAYERS, COLS), (LAYERS, 2, COLS), (LAYERS, 2, COLS), (LAYERS, 1024), (LAYERS, COLS))
    return pl.pallas_call(
        split_small,
        out_shape=[jax.ShapeDtypeStruct((TOK, COLS), BF)] * 2 + [jax.ShapeDtypeStruct(d, F32) for d in shapes],
        in_specs=[vmem] * 3,
        out_specs=[vmem] * 8,
        name="split_small",
    )(hout, gin, sums)


def shards(
    hidden_in, seg_ids, key_mask, w_qkv, qv_bias, w_out, out_bias, ln_gain, ln_shift,
    w_up, up_bias, w_down, down_bias, grad_out,
):
    hout, gin, grad_qkv, grad_out_w, grad_up, grad_down, sums = step_call(
        hidden_in, grad_out, seg_ids.reshape(1, TOK), key_mask.reshape(1, TOK), out_bias, ln_gain, ln_shift, down_bias,
        up_bias, qv_bias, w_qkv.transpose(0, 2, 1, 3), w_out, w_up, w_down,
    )
    hout, gin, qvb, outb, gain, shift, upb, downb = split_call(hout, gin, sums)
    return (
        hout,
        gin,
        grad_qkv.astype(F32).transpose(0, 2, 1, 3),
        qvb,
        grad_out_w.astype(F32),
        outb,
        gain,
        shift,
        grad_up.astype(F32),
        upb,
        grad_down.astype(F32),
        downb,
    )


def solution(mesh):
    tokens = P(("dp", "row"), "col")
    return jax.shard_map(
        shards,
        mesh=mesh,
        in_specs=(
            tokens, P(("dp", "row")), P(("dp", "row")), P(None, "row", None, "col"), P(None, None, "col"),
            P(None, "col", "row"), P(None, "col"), P(None, None, "col"), P(None, None, "col"),
            P(None, "row", "col"), P(None, "col"), P(None, "col", "row"), P(None, "col"), tokens,
        ),
        out_specs=(
            tokens, tokens, P(None, "row", None, "col"), P(None, None, "col"), P(None, "col", "row"),
            P(None, "col"), P(None, None, "col"), P(None, None, "col"), P(None, "row", "col"),
            P(None, "col"), P(None, "col", "row"), P(None, "col"),
        ),
        check_vma=False,
    )
```

time: 281 us -> 239 us (0.85)
  Pallas kernels: 271 us -> 226 us
    pallas_call x1, Pallas kernels: 269 us -> 225 us  [step_call(): pl.pallas_call(kernel, out_shape=[jax.ShapeDtypeStruct((TOK, COLS), BF),...]
where the time goes in v3:
time: 239 us; the launch traced here: 237 us
  Pallas kernels  226 us (95%)
  other arithmetic  9.88 us (4%)
    pallas_call x1, Pallas kernels, step_call(): pl.pallas_call(kernel, out_shape=[jax.ShapeDtypeStruct((TOK, COLS), BF),...  225 us

profile of v3, /device:TPU:0, one launch (start us, length us, event | category | flops | bytes accessed | tf_op | source)
XLA Modules:
  0.0 236.9 jit_solution(1737689402029180964)
XLA Ops:
  0.6 224.6 %encoder_step.1 = (bf16[256,256]{1,0:T(8,128)(2,1)}, bf16[256,256]{1,0:T(8,128)(2,1)}, bf16[2,3,512,256]{3,2,1,0:T(8,128)(2,1)}, bf16[2,256,512]{2,1,0:T(8,128)(...) custom-call(bf16[256,256]{1,0:T(8,128)(2,1)} %hid.1, ...), custom_call_target="tpu_custom_call" | custom-call | tf_op jit(solution)/shard_map/encoder_step/pallas_call | solution.py:782
  225.3 1.7 split_small.1
  227.0 0.0 copy-start
  227.0 4.2 %convert_element_type.11 = f32[2,512,1024]{2,1,0:T(8,128)} convert(bf16[2,512,1024]{2,1,0:T(8,128)(2,1)} %get-tuple-element.38) | non-fusion elementwise | flops 1048576 | bytes 6291456 | tf_op jit(solution)/shard_map/convert_element_type | solution.py:847
  231.2 0.0 copy-done
  231.2 0.0 copy-start.1
  231.2 2.6 %convert_element_type.12 = f32[2,1024,512]{2,1,0:T(8,128)} convert(bf16[2,1024,512]{2,1,0:T(8,128)(2,1)S(1)} %copy-done) | non-fusion elementwise | flops 1048576 | bytes 6291456 | tf_op jit(solution)/shard_map/convert_element_type | solution.py:849
  233.8 0.0 copy-done.1
  233.8 0.0 copy-start.2
  233.8 1.9 convert_bitcast_fusion
  235.8 0.0 copy-done.2
  235.8 1.1 convert_element_type.10
Async XLA Ops:
  227.0 4.2 %copy-start = (bf16[2,1024,512]{2,1,0:T(8,128)(2,1)S(1)}, bf16[2,1024,512]{2,1,0:T(8,128)(2,1)}, u32[]{:S(2)}) copy-start(bf16[2,1024,512]{2,1,0:T(8,128)(2,1)} %get-tuple-element.40) | copy-start | bytes 6291460
  231.2 2.6 %copy-start.1 = (bf16[2,3,512,256]{3,2,1,0:T(8,128)(2,1)S(1)}, bf16[2,3,512,256]{3,2,1,0:T(8,128)(2,1)}, u32[]{:S(2)}) copy-start(bf16[2,3,512,256]{3,2,1,0:T(8,128)(2,1)} %get-tuple-element.32) | copy-start | bytes 4718596
  233.8 2.0 copy-start.2

commit v4 on v3

--- a/solution.py
+++ b/solution.py
@@ -18,7 +18,9 @@
 EPSILON = 1e-05
 MASKED = -1e30
 SCALE = HD**-0.5
-PARTS = ((0, 1, 2, 0), (0, 2, 3, 1), (1, 0, 512, 0), (2, 0, 512, 0), (2, 512, 1024, 1), (3, 0, 256, 0), (3, 256, 512, 1))
+PARTS = (
+    (0, 0, 1, 0), (0, 1, 2, 1), (0, 2, 3, 0), (1, 0, 512, 1), (2, 0, 512, 0), (2, 512, 1024, 1), (3, 0, 256, 0), (3, 256, 512, 1),
+)
 WEIGHT_ROWS = (512, 256, 512, 1024)
 MESH = pl.DeviceIdType.MESH
 BF = jnp.bfloat16
@@ -47,12 +49,12 @@
 def kernel(
     hid, gout, seg, key, outb, gain, shift, downb, upb, qvb, wq, wo, wu, wd,
     hout, gin, gq, go, gu, gd, gsmall,
-    mask, small, WQ, WO, WU, WD, PF, A2H, A2G, S, M, U, GS, GF, F1,
+    mask, small, WQ, WO, WU, WD, PF, A2G, S, M, U, GS, GF, F1,
     STATE, MID, SEC, FIR, QKV, CTX, PR, DG, ACT, NRM, INV, LL, ML, GC,
     PS, XS, L1, L2, HS, HOB, GIB,
     G, RL, R1, A1, R2, A2, R3, FB,
     SGF, SU, SQ, RC, SM, SZ, SY, SR,
-    w_s, w_r, w_rb, wd_s, wd_r, w_lsem, in_s, in_r, ag_s, ag_r, rs_s, rs_r, gr_s, gr_r, out_s, out_r, lsem, sm_s, sm_r,
+    w_s, w_r, w_rb, w_lsem, in_s, in_r, ag_s, ag_r, rs_s, rs_r, gr_s, gr_r, out_s, out_r, lsem, sm_s, sm_r,
 ):
     dp = lax.axis_index("dp")
     row = lax.axis_index("row")
@@ -97,10 +99,16 @@
         to = lax.rem(col + d, 4)
         dev = (dp, row, to)
         return [
-            remote(hid.at[chunk(to)], A2H.at[:, chunk(col, COLS)], in_s.at[0], in_r.at[0], dev),
-            remote(small, PF.at[:, chunk(col, COLS)], in_s.at[1], in_r.at[1], dev),
-            remote(gout.at[chunk(to)], A2G.at[:, chunk(col, COLS)], in_s.at[2], in_r.at[2], dev),
+            remote(small, PF.at[:, chunk(col, COLS)], in_s.at[0], in_r.at[0], dev),
+            remote(gout.at[chunk(to)], A2G.at[:, chunk(col, COLS)], in_s.at[1], in_r.at[1], dev),
         ]
+
+    def hid_block(owner, p):
+        return STATE.at[0, pl.ds(p * 128, 128), chunk(owner, COLS)]
+
+    for p in (0, 1):
+        remote(hid.at[pl.ds(p * 128, 128)], hid_block(col, p), ag_s.at[0], ag_r.at[p], cross_dev).start()
+    remote(hid, STATE.at[0, :, chunk(col, COLS)], ag_s.at[0], ag_r.at[2], core_dev).start()
 
     for l in range(LAYERS):
         rows = (outb[l : l + 1], gain[l, 0:1], shift[l, 0:1], gain[l, 1:2], shift[l, 1:2], downb[l : l + 1])
@@ -108,8 +116,7 @@
             small[l * 8 + r : l * 8 + r + 1, :] = rows[r]
         small[l * 8 + 6 : l * 8 + 8, :] = jnp.zeros((2, COLS), F32)
     for d in (1, 2, 3):
-        for c in in_copies(d)[:2]:
-            c.start()
+        in_copies(d)[0].start()
 
     pairs = ((wq, WQ), (wo, WO), (wu, WU), (wd, WD))
 
@@ -120,9 +127,6 @@
 
     def w_local(l, n):
         return pltpu.make_async_copy(pairs[n][0].at[l], pairs[n][1].at[l, row], w_lsem.at[l, n])
-
-    def w_direct(l, which):
-        return remote(wq.at[l, 0], WQ.at[l, which, 0], wd_s.at[l], wd_r.at[l], row_dev)
 
     def part_axes(p):
         first = PARTS[p][3]
@@ -175,27 +179,24 @@
         w_local(l, n).wait()
         rows = WEIGHT_ROWS[n] * 3 // 4
         if n == 0:
-            w_direct(l, 1 - row).wait_recv()
-            arrived(WQ.at[l, 1 - row, pl.ds(0, 2), pl.ds(0, rows), :], w_rb.at[l, n])
+            arrived(WQ.at[l, 1 - row, :, pl.ds(0, rows), :], w_rb.at[l, n])
         else:
             arrived(pairs[n][1].at[l, 1 - row, pl.ds(0, rows), :], w_rb.at[l, n])
 
     def w_drain(l):
-        w_direct(l, row).wait_send()
-        arrived(WU.at[0, 0, pl.ds(0, 176), pl.ds(0, 512)], w_s.at[l, 0])
-        arrived(WQ.at[0, :, :, pl.ds(0, 176), :], w_s.at[l, 1])
-        arrived(WQ.at[:, :, :, pl.ds(0, 352), :], w_s.at[l, 2])
+        arrived(WU.at[0, 0, pl.ds(0, 192), pl.ds(0, 512)], w_s.at[l, 0])
+        arrived(WQ.at[0, :, :, pl.ds(0, 192), :], w_s.at[l, 1])
+        arrived(WQ.at[:, :, :, pl.ds(0, 384), :], w_s.at[l, 2])
 
     parts = range(len(PARTS))
     for p in parts:
         w_piece(0, p, row).start()
-    w_direct(0, row).start()
     for n in range(4):
         w_local(0, n).start()
     for p in parts:
         w_step_one(0, p)
     for d in (1, 2, 3):
-        in_copies(d)[2].start()
+        in_copies(d)[1].start()
     for n in range(4):
         w_local(1, n).start()
 
@@ -205,16 +206,22 @@
     keep = jnp.where(same_place, 1.0, key_lanes)
     mask[...] = jnp.where(seg_lanes.T == seg_lanes, keep, 0.0)
 
-    A2H[:, chunk(col, COLS)] = hid[chunk(col), :]
     A2G[:, chunk(col, COLS)] = gout[chunk(col), :]
     PF[:, chunk(col, COLS)] = small[...]
-    arrived(A2H.at[:, pl.ds(0, 3 * COLS)], in_r.at[0])
-    arrived(PF.at[:, pl.ds(0, 3 * COLS)], in_r.at[1])
-    arrived(A2G.at[:, pl.ds(0, 3 * COLS)], in_r.at[2])
-    S[...] = A2H[...].astype(F32)
+    STATE[0, :, chunk(col, COLS)] = hid[...]
+    for p in parts[:3]:
+        w_step_two(0, p)
+    for p in (0, 1):
+        arrived(hid_block(col_cross, p), ag_r.at[p])
+        remote(hid_block(col_cross, p), hid_block(col_cross, p), ag_s.at[0], ag_r.at[3], core_dev).start()
+    for p in parts[3:]:
+        w_step_two(0, p)
+    arrived(STATE.at[0, :, chunk(col_core, COLS)], ag_r.at[2])
+    arrived(STATE.at[0, :, chunk(col_diag, COLS)], ag_r.at[3])
+    S[...] = STATE[0, chunk(col), :].astype(F32)
+    arrived(PF.at[:, pl.ds(0, 3 * COLS)], in_r.at[0])
+    arrived(A2G.at[:, pl.ds(0, 3 * COLS)], in_r.at[1])
     U[...] = A2G[...].astype(F32)
-    w_step_two(0, 0)
-    w_step_two(0, 1)
 
     def ag_rows(owner, p):
         return pl.ds(pl.multiple_of(owner * OWN + p * 32, 32), 32)
@@ -428,19 +435,18 @@
 
     def forward(l, carry):
         X = STATE.at[l]
-        X[chunk(col), :] = S[...].astype(BF)
-        ag_start(X)
-
-        @pl.when(l == 0)
+
+        @pl.when(l > 0)
         def _():
-            for p in parts[2:]:
-                w_step_two(0, p)
-            for p in parts:
-                w_piece(1, p, row).start()
-            w_direct(1, row).start()
+            X[chunk(col), :] = S[...].astype(BF)
+            ag_start(X)
 
         w_wait(l, 0)
-        ag_finish(X)
+
+        @pl.when(l > 0)
+        def _():
+            ag_finish(X)
+
         for j in range(3):
             mixed = dot(STATE[l, :, :512], WQ[l, 0, j]) + dot(STATE[l, :, 512:], WQ[l, 1, j])
             if j != 1:
@@ -451,7 +457,7 @@
         @pl.when(l == 0)
         def _():
             for p in parts:
-                w_step_one(1, p)
+                w_piece(1, p, row).start()
 
         for h in range(HEADS_LOCAL):
             lanes = slice(h * HD, (h + 1) * HD)
@@ -461,12 +467,6 @@
             probs = raised / jnp.sum(raised, axis=1, keepdims=True)
             PR[l, h] = probs
             CTX[l, :, lanes] = dot(probs.astype(BF), QKV[l, 2, :, lanes]).astype(BF)
-
-        @pl.when(l == 0)
-        def _():
-            for p in parts:
-                w_step_two(1, p)
-
         w_wait(l, 1)
         for h in (0, 1):
             PS[:, half(h)] = dot(CTX[l], WO[l, h]).astype(BF)
@@ -481,6 +481,12 @@
         X = MID.at[l]
         X[chunk(col), :] = middle.astype(BF)
         ag_start(X)
+
+        @pl.when(l == 0)
+        def _():
+            for p in parts:
+                w_step_one(1, p)
+
         w_wait(l, 2)
         ag_finish(X)
 
@@ -496,6 +502,12 @@
 
         lax.fori_loop(0, 4, lift, 0)
         ag_drain(X)
+
+        @pl.when(l == 0)
+        def _():
+            for p in parts:
+                w_step_two(1, p)
+
         w_wait(l, 3)
         for h in (0, 1):
             for q in (0, 1):
@@ -732,9 +744,8 @@
     gin[...] = GIB[...]
     both(t5b, 0, 4)
 
-    arrived(A2H.at[:, pl.ds(0, 3 * COLS)], in_s.at[0])
-    arrived(PF.at[:, pl.ds(0, 3 * COLS)], in_s.at[1])
-    arrived(A2G.at[:, pl.ds(0, 3 * COLS)], in_s.at[2])
+    arrived(PF.at[:, pl.ds(0, 3 * COLS)], in_s.at[0])
+    arrived(A2G.at[:, pl.ds(0, 3 * COLS)], in_s.at[1])
     for n in (0, 1):
         arrived(HOB.at[pl.ds(0, 3 * OWN)], out_s.at[n])
     arrived(RC, sm_s.at[0])
@@ -761,7 +772,7 @@
     scratch = [
         V((TOK, TOK), F32), V((16, COLS), F32),
         V((L, 2, 3, 512, COLS), BF), V((L, 2, 256, 512), BF), V((L, 2, 512, 1024), BF), V((L, 2, 1024, 512), BF),
-        V((16, 1024), F32), V((OWN, D), BF), V((OWN, D), BF),
+        V((16, 1024), F32), V((OWN, D), BF),
         V((OWN, D), F32), V((OWN, D), F32), V((OWN, D), F32), V((OWN, D), F32), V((OWN, D), F32), V((OWN, D), F32),
         V((L, TOK, D), BF), V((L, TOK, D), BF), V((TOK, D), BF), V((TOK, D), BF),
         V((L, 3, TOK, COLS), BF), V((L, TOK, COLS), BF), V((L, HEADS_LOCAL, TOK, TOK), F32),
@@ -775,7 +786,7 @@
         V((L, SLABS, 128, 512), BF),
         V((L, 8, D), F32), V((L, 1, 1024), F32), V((L, 2, COLS), F32), V((3, L, 8, COLS), F32),
         V((32, COLS), F32), V((4, 32, COLS), F32), V((4, 32, COLS), F32), V((32, COLS), F32),
-        dma((L, 3)), dma((L, 7, 2)), dma((L, 4)), dma((L,)), dma((L,)), dma((L, 4)), dma((3,)), dma((3,)),
+        dma((L, 3)), dma((L, len(PARTS), 2)), dma((L, 4)), dma((L, 4)), dma((2,)), dma((2,)),
         dma((1,)), dma((4,)), dma((1,)), dma((6,)),
         dma((L, 7)), dma((L, SLABS, 7)), dma((2,)), dma((2,)), dma((L,)), dma((4,)), dma((4,)),
     ]
@@ -800,7 +811,24 @@
     )(*args)
 
 
-def split_small(hout, gin, sums, out_h, out_g, qvb, outb, gain, shift, upb, downb):
+def finish_kernel(
+    hout, gin, sums, gq, go, gu, gd,
+    out_h, out_g, qvb, outb, gain, shift, upb, downb, fq, fo, fu, fd,
+    low, high, low_q, high_q, in_sem, out_sem,
+):
+    blocks = []
+    for l in range(LAYERS):
+        for j in range(3):
+            blocks.append((gq.at[l, j], fq.at[l, j], low_q.at[l * 3 + j], high_q.at[l * 3 + j]))
+    n = 0
+    for l in range(LAYERS):
+        places = [(gd, fd, (l, pl.ds(q * 256, 256))) for q in range(4)] + [(go, fo, (l,))]
+        places += [(gu, fu, (l, pl.ds(q * 256, 256), pl.ds(h * 512, 512))) for q in range(2) for h in range(2)]
+        for src, dst, where in places:
+            blocks.append((src.at[where], dst.at[where], low.at[n], high.at[n]))
+            n += 1
+    for k, (src, _, here, _) in enumerate(blocks):
+        pltpu.make_async_copy(src, here, in_sem.at[k]).start()
     out_h[...] = hout[...]
     out_g[...] = gin[...]
     for l in range(LAYERS):
@@ -812,18 +840,33 @@
         for q in range(4):
             upb[l : l + 1, q * COLS : (q + 1) * COLS] = sums[16 + 4 * l + q : 17 + 4 * l + q, :]
         qvb[l] = sums[24 + 2 * l : 26 + 2 * l, :]
-
-
-def split_call(hout, gin, sums):
+    for k, (src, dst, here, wide) in enumerate(blocks):
+        pltpu.make_async_copy(src, here, in_sem.at[k]).wait()
+        wide[...] = here[...].astype(F32)
+        pltpu.make_async_copy(wide, dst, out_sem.at[k]).start()
+    for k, (_, dst, _, wide) in enumerate(blocks):
+        pltpu.make_async_copy(wide, dst, out_sem.at[k]).wait()
+
+
+def finish_call(*args):
     vmem = pl.BlockSpec(memory_space=pltpu.VMEM)
-    shapes = ((LAYERS, 2, COLS), (LAYERS, COLS), (LAYERS, 2, COLS), (LAYERS, 2, COLS), (LAYERS, 1024), (LAYERS, COLS))
+    hbm = pl.BlockSpec(memory_space=pl.ANY)
+    L = LAYERS
+    small = ((L, 2, COLS), (L, COLS), (L, 2, COLS), (L, 2, COLS), (L, 1024), (L, COLS))
+    large = ((L, 3, 512, COLS), (L, 256, 512), (L, 512, 1024), (L, 1024, 512))
     return pl.pallas_call(
-        split_small,
-        out_shape=[jax.ShapeDtypeStruct((TOK, COLS), BF)] * 2 + [jax.ShapeDtypeStruct(d, F32) for d in shapes],
-        in_specs=[vmem] * 3,
-        out_specs=[vmem] * 8,
-        name="split_small",
-    )(hout, gin, sums)
+        finish_kernel,
+        out_shape=[jax.ShapeDtypeStruct((TOK, COLS), BF)] * 2 + [jax.ShapeDtypeStruct(d, F32) for d in small + large],
+        in_specs=[vmem] * 3 + [hbm] * 4,
+        out_specs=[vmem] * 8 + [hbm] * 4,
+        scratch_shapes=[
+            pltpu.VMEM((9 * L, 256, 512), BF), pltpu.VMEM((9 * L, 256, 512), F32),
+            pltpu.VMEM((3 * L, 512, COLS), BF), pltpu.VMEM((3 * L, 512, COLS), F32),
+            pltpu.SemaphoreType.DMA((12 * L,)), pltpu.SemaphoreType.DMA((12 * L,)),
+        ],
+        compiler_params=pltpu.CompilerParams(vmem_limit_bytes=32 * 2**20),
+        name="finish",
+    )(*args)
 
 
 def shards(
@@ -834,20 +877,11 @@
         hidden_in, grad_out, seg_ids.reshape(1, TOK), key_mask.reshape(1, TOK), out_bias, ln_gain, ln_shift, down_bias,
         up_bias, qv_bias, w_qkv.transpose(0, 2, 1, 3), w_out, w_up, w_down,
     )
-    hout, gin, qvb, outb, gain, shift, upb, downb = split_call(hout, gin, sums)
+    hout, gin, qvb, outb, gain, shift, upb, downb, grad_qkv, grad_out_w, grad_up, grad_down = finish_call(
+        hout, gin, sums, grad_qkv, grad_out_w, grad_up, grad_down
+    )
     return (
-        hout,
-        gin,
-        grad_qkv.astype(F32).transpose(0, 2, 1, 3),
-        qvb,
-        grad_out_w.astype(F32),
-        outb,
-        gain,
-        shift,
-        grad_up.astype(F32),
-        upb,
-        grad_down.astype(F32),
-        downb,
+        hout, gin, grad_qkv.transpose(0, 2, 1, 3), qvb, grad_out_w, outb, gain, shift, grad_up, upb, grad_down, downb,
     )
 
 

time: 239 us -> 228 us (0.954)
  other arithmetic: 9.88 us -> 0 us
  local copies, waits for them, and re-layouts: 0.01 us -> 8.19 us
  Pallas kernels: 226 us -> 219 us
    pallas_call x1, Pallas kernels: 225 us -> 212 us  [step_call(): pl.pallas_call(kernel, out_shape=[jax.ShapeDtypeStruct((TOK, COLS), BF),...]
    unnamed x6 -> x14, local copies, waits for them, and re-layouts: 0.01 us -> 8.19 us
    convert_element_type x3 -> x0, other arithmetic: 7.93 us -> none  [the longest x1 4.22 us: shards(): grad_up.astype(F32)]
    pallas_call x1, Pallas kernels: 1.7 us -> 6.18 us  [finish_call(): pl.pallas_call(finish_kernel, out_shape=[jax.ShapeDtypeStruct((TOK, COLS)...]
where the time goes in v4:
time: 228 us; the launch traced here: 227 us
  Pallas kernels  219 us (96%)
  local copies, waits for them, and re-layouts  8.19 us (4%)
    pallas_call x1, Pallas kernels, step_call(): pl.pallas_call(kernel, out_shape=[jax.ShapeDtypeStruct((TOK, COLS), BF),...  212 us
    unnamed x14, local copies, waits for them, and re-layouts  8.19 us
    pallas_call x1, Pallas kernels, finish_call(): pl.pallas_call(finish_kernel, out_shape=[jax.ShapeDtypeStruct((TOK, COLS)...  6.18 us

profile of v4, /device:TPU:0, one launch (start us, length us, event | category | flops | bytes accessed | tf_op | source)
XLA Modules:
  0.0 227.4 jit_solution(3009144206858746115)
XLA Ops:
  0.6 212.4 %encoder_step.1 = (bf16[256,256]{1,0:T(8,128)(2,1)}, bf16[256,256]{1,0:T(8,128)(2,1)}, bf16[2,3,512,256]{3,2,1,0:T(8,128)(2,1)}, bf16[2,256,512]{2,1,0:T(8,128)(...) custom-call(bf16[256,256]{1,0:T(8,128)(2,1)} %hid.1, ...), custom_call_target="tpu_custom_call" | custom-call | tf_op jit(solution)/shard_map/encoder_step/pallas_call | solution.py:793
  213.0 0.0 copy-start
  213.0 1.6 copy-done
  214.6 0.0 copy-start.1
  214.6 1.6 copy-done.1
  216.2 0.0 copy-start.2
  216.2 1.4 copy-done.2
  217.6 0.0 copy-start.3
  217.6 1.0 copy-done.3
  218.7 0.0 copy-start.4
  218.7 0.9 copy-done.4
  219.6 0.0 copy-start.5
  219.6 0.9 copy-done.5
  220.5 0.0 copy-start.6
  220.5 0.8 copy-done.6
  221.2 6.2 %finish.1 = (bf16[256,256]{1,0:T(8,128)(2,1)}, bf16[256,256]{1,0:T(8,128)(2,1)}, f32[2,2,256]{2,1,0:T(2,128)}, f32[2,256]{1,0:T(2,128)}, f32[2,2,256]{2,1,0:T(2,...) custom-call(bf16[256,256]{1,0:T(8,128)(2,1)S(1)} %copy-done.4, ...), custom_call_target="tpu_custom_call" | custom-call | tf_op jit(solution)/shard_map/finish/pallas_call | solution.py:857
Async XLA Ops:
  213.0 1.6 copy-start
  214.6 1.6 copy-start.1
  216.2 1.4 copy-start.2
  217.6 1.0 copy-start.3
  218.7 0.9 copy-start.4
  219.6 0.9 copy-start.5
  220.5 0.8 copy-start.6

commit v5 on v4

--- a/solution.py
+++ b/solution.py
@@ -106,18 +106,6 @@
     def hid_block(owner, p):
         return STATE.at[0, pl.ds(p * 128, 128), chunk(owner, COLS)]
 
-    for p in (0, 1):
-        remote(hid.at[pl.ds(p * 128, 128)], hid_block(col, p), ag_s.at[0], ag_r.at[p], cross_dev).start()
-    remote(hid, STATE.at[0, :, chunk(col, COLS)], ag_s.at[0], ag_r.at[2], core_dev).start()
-
-    for l in range(LAYERS):
-        rows = (outb[l : l + 1], gain[l, 0:1], shift[l, 0:1], gain[l, 1:2], shift[l, 1:2], downb[l : l + 1])
-        for r in range(6):
-            small[l * 8 + r : l * 8 + r + 1, :] = rows[r]
-        small[l * 8 + 6 : l * 8 + 8, :] = jnp.zeros((2, COLS), F32)
-    for d in (1, 2, 3):
-        in_copies(d)[0].start()
-
     pairs = ((wq, WQ), (wo, WO), (wu, WU), (wd, WD))
 
     def region(ref, n, lo, hi, rows):
@@ -189,28 +177,42 @@
         arrived(WQ.at[:, :, :, pl.ds(0, 384), :], w_s.at[l, 2])
 
     parts = range(len(PARTS))
-    for p in parts:
+    for p in parts[:3]:
+        w_piece(0, p, row).start()
+    for p in (0, 1):
+        remote(hid.at[pl.ds(p * 128, 128)], hid_block(col, p), ag_s.at[0], ag_r.at[p], cross_dev).start()
+    remote(hid, STATE.at[0, :, chunk(col, COLS)], ag_s.at[0], ag_r.at[2], core_dev).start()
+    for p in parts[3:]:
         w_piece(0, p, row).start()
     for n in range(4):
         w_local(0, n).start()
-    for p in parts:
+    for l in range(LAYERS):
+        rows = (outb[l : l + 1], gain[l, 0:1], shift[l, 0:1], gain[l, 1:2], shift[l, 1:2], downb[l : l + 1])
+        for r in range(6):
+            small[l * 8 + r : l * 8 + r + 1, :] = rows[r]
+        small[l * 8 + 6 : l * 8 + 8, :] = jnp.zeros((2, COLS), F32)
+    for d in (1, 2, 3):
+        in_copies(d)[0].start()
+    for p in parts[:3]:
+        w_step_one(0, p)
+
+    seg_lanes = jnp.broadcast_to(seg[...].astype(F32), (TOK, TOK))
+    key_lanes = jnp.broadcast_to(key[...].astype(F32), (TOK, TOK))
+    same_place = lax.broadcasted_iota(jnp.int32, (TOK, TOK), 0) == lax.broadcasted_iota(jnp.int32, (TOK, TOK), 1)
+    keep = jnp.where(same_place, 1.0, key_lanes)
+    mask[...] = jnp.where(seg_lanes.T == seg_lanes, keep, 0.0)
+
+    A2G[:, chunk(col, COLS)] = gout[chunk(col), :]
+    PF[:, chunk(col, COLS)] = small[...]
+    STATE[0, :, chunk(col, COLS)] = hid[...]
+    for p in parts[:3]:
+        w_step_two(0, p)
+    for p in parts[3:]:
         w_step_one(0, p)
     for d in (1, 2, 3):
         in_copies(d)[1].start()
     for n in range(4):
         w_local(1, n).start()
-
-    seg_lanes = jnp.broadcast_to(seg[...].astype(F32), (TOK, TOK))
-    key_lanes = jnp.broadcast_to(key[...].astype(F32), (TOK, TOK))
-    same_place = lax.broadcasted_iota(jnp.int32, (TOK, TOK), 0) == lax.broadcasted_iota(jnp.int32, (TOK, TOK), 1)
-    keep = jnp.where(same_place, 1.0, key_lanes)
-    mask[...] = jnp.where(seg_lanes.T == seg_lanes, keep, 0.0)
-
-    A2G[:, chunk(col, COLS)] = gout[chunk(col), :]
-    PF[:, chunk(col, COLS)] = small[...]
-    STATE[0, :, chunk(col, COLS)] = hid[...]
-    for p in parts[:3]:
-        w_step_two(0, p)
     for p in (0, 1):
         arrived(hid_block(col_cross, p), ag_r.at[p])
         remote(hid_block(col_cross, p), hid_block(col_cross, p), ag_s.at[0], ag_r.at[3], core_dev).start()
@@ -238,13 +240,21 @@
         for c in ag_send(X):
             c.start()
 
-    def ag_finish(X):
+    def ag_near(X):
+        arrived(X.at[chunk(col_core)], ag_r.at[2])
+
+    def ag_far(X):
         for p in (0, 1):
             rows = ag_rows(col_cross, p)
             arrived(X.at[rows], ag_r.at[p])
             remote(X.at[rows], X.at[rows], ag_s.at[0], ag_r.at[3], core_dev).start()
-        arrived(X.at[chunk(col_core)], ag_r.at[2])
         arrived(X.at[chunk(col_diag)], ag_r.at[3])
+
+    def ag_finish(X):
+        ag_far(X)
+        ag_near(X)
+
+    near_rows, far_rows = chunk(xh, 2 * OWN), chunk(1 - xh, 2 * OWN)
 
     def ag_drain(X):
         arrived(X.at[pl.ds(0, 3 * OWN)], ag_s.at[0])
@@ -263,6 +273,10 @@
 
     def rs_send(par, h):
         for t in (0, 1):
+            rs_first(par, h, t).start()
+
+    def rs_send_rows(par, t):
+        for h in (0, 1):
             rs_first(par, h, t).start()
 
     def rs_mid(par, h):
@@ -443,15 +457,24 @@
 
         w_wait(l, 0)
 
+        def project(rows):
+            for j in range(3):
+                mixed = dot(STATE[l, rows, :512], WQ[l, 0, j]) + dot(STATE[l, rows, 512:], WQ[l, 1, j])
+                if j != 1:
+                    mixed = mixed + qvb[l, j // 2 : j // 2 + 1, :]
+                QKV[l, j, rows, :] = mixed.astype(BF)
+
         @pl.when(l > 0)
         def _():
-            ag_finish(X)
-
-        for j in range(3):
-            mixed = dot(STATE[l, :, :512], WQ[l, 0, j]) + dot(STATE[l, :, 512:], WQ[l, 1, j])
-            if j != 1:
-                mixed = mixed + qvb[l, j // 2 : j // 2 + 1, :]
-            QKV[l, j] = mixed.astype(BF)
+            ag_near(X)
+
+        project(near_rows)
+
+        @pl.when(l > 0)
+        def _():
+            ag_far(X)
+
+        project(far_rows)
         ag_drain(X)
 
         @pl.when(l == 0)
@@ -468,9 +491,10 @@
             PR[l, h] = probs
             CTX[l, :, lanes] = dot(probs.astype(BF), QKV[l, 2, :, lanes]).astype(BF)
         w_wait(l, 1)
-        for h in (0, 1):
-            PS[:, half(h)] = dot(CTX[l], WO[l, h]).astype(BF)
-            rs_send(0, h)
+        for t, rows in ((0, far_rows), (1, near_rows)):
+            for h in (0, 1):
+                PS[rows, half(h)] = dot(CTX[l, rows, :], WO[l, h]).astype(BF)
+            rs_send_rows(0, t)
         rs_mid(0, 0)
         rs_mid(0, 1)
         for h in (0, 1):
@@ -488,19 +512,24 @@
                 w_step_one(1, p)
 
         w_wait(l, 2)
-        ag_finish(X)
-
-        def lift(n, c):
-            lanes = chunk(n, COLS)
-            lifted = dot(MID[l, :, :512], WU[l, 0, :, lanes]) + dot(MID[l, :, 512:], WU[l, 1, :, lanes])
-            lifted = lifted + upb[pl.ds(l, 1), lanes]
-            phi = 0.5 * (1.0 + lax.erf(lifted * (0.5**0.5)))
-            density = jnp.exp(-0.5 * lifted * lifted) * 0.3989422804014327
-            DG[l, :, lanes] = phi + lifted * density
-            ACT[l, :, lanes] = (lifted * phi).astype(BF)
-            return c
-
-        lax.fori_loop(0, 4, lift, 0)
+
+        def lift_rows(rows):
+            def lift(n, c):
+                lanes = chunk(n, COLS)
+                lifted = dot(MID[l, rows, :512], WU[l, 0, :, lanes]) + dot(MID[l, rows, 512:], WU[l, 1, :, lanes])
+                lifted = lifted + upb[pl.ds(l, 1), lanes]
+                phi = 0.5 * (1.0 + lax.erf(lifted * (0.5**0.5)))
+                density = jnp.exp(-0.5 * lifted * lifted) * 0.3989422804014327
+                DG[l, rows, lanes] = phi + lifted * density
+                ACT[l, rows, lanes] = (lifted * phi).astype(BF)
+                return c
+
+            lax.fori_loop(0, 4, lift, 0)
+
+        ag_near(X)
+        lift_rows(near_rows)
+        ag_far(X)
+        lift_rows(far_rows)
         ag_drain(X)
 
         @pl.when(l == 0)
@@ -509,11 +538,12 @@
                 w_step_two(1, p)
 
         w_wait(l, 3)
-        for h in (0, 1):
-            for q in (0, 1):
-                lanes = pl.ds(h * 512 + q * 256, 256)
-                PS[:, lanes] = dot(ACT[l], WD[l, h, :, pl.ds(q * 256, 256)]).astype(BF)
-            rs_send(1, h)
+        for t, rows in ((0, far_rows), (1, near_rows)):
+            for h in (0, 1):
+                for q in (0, 1):
+                    lanes = pl.ds(h * 512 + q * 256, 256)
+                    PS[rows, lanes] = dot(ACT[l, rows, :], WD[l, h, :, pl.ds(q * 256, 256)]).astype(BF)
+            rs_send_rows(1, t)
         rs_mid(1, 0)
         rs_mid(1, 1)
         for h in (0, 1):
@@ -551,11 +581,20 @@
 
         @pl.when(i > 0)
         def _():
-            both(t2, prev, 2)
-            both(t3, prev, 0)
-            both(t1b, prev, 4)
+            both(t4, prev, 0)
+            both(t3, prev, 2)
 
         ag_finish(SEC)
+
+        def down_grad(f, c):
+            total = dot_tn(ACT[l, :, chunk(f, COLS)], SEC[...]).astype(BF)
+            rows = chunk(lax.rem(f, 2), COLS)
+            for r in (0, 1):
+                G[l, lax.div(f, 2), r, rows, :] = total[:, r * 512 : (r + 1) * 512]
+            return c
+
+        lax.fori_loop(0, 4, down_grad, 0)
+        both(t1, l, 0)
 
         def pull(n, c):
             lanes = chunk(n, COLS)
@@ -566,6 +605,12 @@
             return c
 
         lax.fori_loop(0, 4, pull, 0)
+        ag_drain(SEC)
+
+        @pl.when(i > 0)
+        def _():
+            both(t2, prev, 4)
+
         for h in (0, 1):
             for q in (0, 1):
                 lanes = pl.ds(h * 512 + q * 256, 256)
@@ -574,22 +619,23 @@
         rs_mid(0, 0)
         rs_mid(0, 1)
 
-        def down_grad(f, c):
-            total = dot_tn(ACT[l, :, chunk(f, COLS)], SEC[...]).astype(BF)
-            rows = chunk(lax.rem(f, 2), COLS)
+        def up_grad(n, c):
+            total = dot_tn(MID[l, :, chunk(n, COLS)], LL[...]).astype(BF)
+            rows = chunk(lax.rem(n, 2), COLS)
             for r in (0, 1):
-                G[l, lax.div(f, 2), r, rows, :] = total[:, r * 512 : (r + 1) * 512]
+                G[l, 2 + r, lax.div(n, 2), rows, :] = total[:, r * 512 : (r + 1) * 512]
             return c
 
-        lax.fori_loop(0, 4, down_grad, 0)
-        both(t1, l, 0)
-        ag_drain(SEC)
+        lax.fori_loop(0, 4, up_grad, 0)
+        both(t1, l, 2)
+
+        both(t1b, l, 0)
 
         @pl.when(i > 0)
         def _():
-            both(t4, prev, 0)
-            both(t3, prev, 2)
-            both(t2, prev, 4)
+            both(t4, prev, 2)
+            both(t3, prev, 4)
+
 
         for h in (0, 1):
             GS[:, half(h)] = GS[:, half(h)] + rs_end(0, h)
@@ -604,23 +650,9 @@
         FIR[chunk(col), :] = grad_first.astype(BF)
         ag_start(FIR)
 
-        def up_grad(n, c):
-            total = dot_tn(MID[l, :, chunk(n, COLS)], LL[...]).astype(BF)
-            rows = chunk(lax.rem(n, 2), COLS)
-            for r in (0, 1):
-                G[l, 2 + r, lax.div(n, 2), rows, :] = total[:, r * 512 : (r + 1) * 512]
-            return c
-
-        lax.fori_loop(0, 4, up_grad, 0)
-        both(t1, l, 2)
-
         @pl.when(i > 0)
         def _():
-            both(t5, prev, 0)
-            both(t4, prev, 2)
-            both(t3, prev, 4)
-
-        both(t1b, l, 0)
+            both(t4, prev, 4)
 
         ag_finish(FIR)
         GC[...] = (dot_nt(FIR[:, :512], WO[l, 0]) + dot_nt(FIR[:, 512:], WO[l, 1])).astype(BF)
@@ -638,6 +670,25 @@
             ML[:, h * HD : (h + 1) * HD] = grad_query.astype(BF)
             ML[:, COLS + h * HD : COLS + (h + 1) * HD] = grad_key.astype(BF)
             ML[:, 2 * COLS + h * HD : 2 * COLS + (h + 1) * HD] = grad_value.astype(BF)
+        ag_drain(FIR)
+        total = dot_tn(CTX[l], FIR[...]).astype(BF)
+        for r in (0, 1):
+            for q in range(4):
+                G[l, 5, r, q * 128 : q * 128 + 64, :] = total[q * 64 : (q + 1) * 64, r * 512 : (r + 1) * 512]
+
+        def qkv_grad(r, c):
+            for q in (0, 1):
+                total = dot_tn(STATE[l, :, chunk(2 * r + q, COLS)], ML[...]).astype(BF)
+                G[l, 4, r, q * 256 : (q + 1) * 256, :] = total[:, :512]
+                for b in range(4):
+                    G[l, 5, r, b * 128 + 64 : b * 128 + 128, q * 256 : (q + 1) * 256] = total[b * 64 : (b + 1) * 64, 512:]
+            return c
+
+        lax.fori_loop(0, 2, qkv_grad, 0)
+        both(t1, l, 4)
+        both(t1b, l, 2)
+        both(t2, l, 0)
+
         for h in (0, 1):
             for q in (0, 1):
                 lanes = pl.ds(h * 512 + q * 256, 256)
@@ -647,30 +698,9 @@
             rs_send(1, h)
         rs_mid(1, 0)
         rs_mid(1, 1)
-        total = dot_tn(CTX[l], FIR[...]).astype(BF)
-        for r in (0, 1):
-            for q in range(4):
-                G[l, 5, r, q * 128 : q * 128 + 64, :] = total[q * 64 : (q + 1) * 64, r * 512 : (r + 1) * 512]
-
-        def qkv_grad(r, c):
-            for q in (0, 1):
-                total = dot_tn(STATE[l, :, chunk(2 * r + q, COLS)], ML[...]).astype(BF)
-                G[l, 4, r, q * 256 : (q + 1) * 256, :] = total[:, :512]
-                for b in range(4):
-                    G[l, 5, r, b * 128 + 64 : b * 128 + 128, q * 256 : (q + 1) * 256] = total[b * 64 : (b + 1) * 64, 512:]
-            return c
-
-        lax.fori_loop(0, 2, qkv_grad, 0)
-        both(t1, l, 4)
-        ag_drain(FIR)
-        both(t1b, l, 2)
-        both(t2, l, 0)
-
-        @pl.when(i > 0)
-        def _():
-            both(t5, prev, 2)
-            both(t4, prev, 4)
-            both(t5b, prev, 0)
+        both(t3, l, 0)
+        both(t2, l, 2)
+        both(t1b, l, 4)
 
         for h in (0, 1):
             U[:, half(h)] = GF[:, half(h)] + rs_end(1, h)
@@ -699,11 +729,12 @@
 
     for d in (1, 2, 3):
         sc_copy(d).start()
-    both(t2, 0, 2)
-    both(t5b, 1, 2)
+    both(t5, 1, 0)
+    both(t5, 1, 2)
+    both(t4, 0, 0)
+    both(t3, 0, 2)
+    both(t2, 0, 4)
     both(t5, 1, 4)
-    both(t3, 0, 0)
-    both(t1b, 0, 4)
     arrived(RC, sm_r.at[0])
     feature = SGF[:, :, chunk(col, COLS)]
     for d in (0, 1, 2):
@@ -716,27 +747,26 @@
     SZ[z, 28:32, :] = jnp.zeros((4, COLS), F32)
     for d in (1, 2, 3):
         sd_copy(0, d, z).start()
-    both(t4, 0, 0)
-    both(t3, 0, 2)
-    both(t2, 0, 4)
-    both(t5b, 1, 4)
+    both(t3, 0, 4)
+    both(t4, 0, 2)
+    both(t5, 0, 0)
+    both(t5b, 1, 0)
+    both(t5b, 1, 2)
     arrived(SZ.at[pl.ds(0, 3)], sm_r.at[1])
     SY[y] = SZ[0] + SZ[1] + SZ[2] + SZ[3]
     for d in (1, 2, 3):
         sd_copy(1, d, y).start()
-    both(t5, 0, 0)
-    both(t4, 0, 2)
-    both(t3, 0, 4)
+    both(t4, 0, 4)
+    both(t5, 0, 2)
+    both(t5b, 1, 4)
     arrived(SY.at[pl.ds(0, 3)], sm_r.at[2])
     SM[...] = SY[0] + SY[1] + SY[2] + SY[3]
     sr_copy().start()
+    both(t5, 0, 4)
     both(t5b, 0, 0)
-    both(t5, 0, 2)
-    both(t4, 0, 4)
+    both(t5b, 0, 2)
     sr_copy().wait_recv()
     gsmall[...] = SM[...] + SR[...]
-    both(t5b, 0, 2)
-    both(t5, 0, 4)
     for n in (0, 1):
         buf = (HOB, GIB)[n]
         arrived(buf.at[pl.ds(0, 3 * OWN)], out_r.at[n])

time: 228 us -> 225 us (0.987)
  Pallas kernels: 219 us -> 215 us
    pallas_call x1, Pallas kernels: 212 us -> 209 us  [step_call(): pl.pallas_call(kernel, out_shape=[jax.ShapeDtypeStruct((TOK, COLS), BF),...]
where the time goes in v5:
time: 225 us; the launch traced here: 224 us
  Pallas kernels  215 us (96%)
  local copies, waits for them, and re-layouts  8.19 us (4%)
    pallas_call x1, Pallas kernels, step_call(): pl.pallas_call(kernel, out_shape=[jax.ShapeDtypeStruct((TOK, COLS), BF),...  209 us
    unnamed x14, local copies, waits for them, and re-layouts  8.19 us
    pallas_call x1, Pallas kernels, finish_call(): pl.pallas_call(finish_kernel, out_shape=[jax.ShapeDtypeStruct((TOK, COLS)...  6.18 us

profile of v5, /device:TPU:0, one launch (start us, length us, event | category | flops | bytes accessed | tf_op | source)
XLA Modules:
  0.0 224.1 jit_solution(3144397515024906785)
XLA Ops:
  0.6 209.1 %encoder_step.1 = (bf16[256,256]{1,0:T(8,128)(2,1)}, bf16[256,256]{1,0:T(8,128)(2,1)}, bf16[2,3,512,256]{3,2,1,0:T(8,128)(2,1)}, bf16[2,256,512]{2,1,0:T(8,128)(...) custom-call(bf16[256,256]{1,0:T(8,128)(2,1)} %hid.1, ...), custom_call_target="tpu_custom_call" | custom-call | tf_op jit(solution)/shard_map/encoder_step/pallas_call | solution.py:823
  209.7 0.0 copy-start
  209.7 1.6 copy-done
  211.3 0.0 copy-start.1
  211.3 1.6 copy-done.1
  212.9 0.0 copy-start.2
  212.9 1.4 copy-done.2
  214.3 0.0 copy-start.3
  214.3 1.0 copy-done.3
  215.4 0.0 copy-start.4
  215.4 0.9 copy-done.4
  216.3 0.0 copy-start.5
  216.3 0.9 copy-done.5
  217.2 0.0 copy-start.6
  217.2 0.8 copy-done.6
  217.9 6.2 %finish.1 = (bf16[256,256]{1,0:T(8,128)(2,1)}, bf16[256,256]{1,0:T(8,128)(2,1)}, f32[2,2,256]{2,1,0:T(2,128)}, f32[2,256]{1,0:T(2,128)}, f32[2,2,256]{2,1,0:T(2,...) custom-call(bf16[256,256]{1,0:T(8,128)(2,1)S(1)} %copy-done.4, ...), custom_call_target="tpu_custom_call" | custom-call | tf_op jit(solution)/shard_map/finish/pallas_call | solution.py:887
Async XLA Ops:
  209.7 1.6 copy-start
  211.3 1.6 copy-start.1
  212.9 1.4 copy-start.2
  214.3 1.0 copy-start.3
  215.4 0.9 copy-start.4
  216.3 0.9 copy-start.5
  217.2 0.8 copy-start.6

commit v6 on v5

--- a/solution.py
+++ b/solution.py
@@ -653,6 +653,7 @@
         @pl.when(i > 0)
         def _():
             both(t4, prev, 4)
+            both(t5, prev, 0)
 
         ag_finish(FIR)
         GC[...] = (dot_nt(FIR[:, :512], WO[l, 0]) + dot_nt(FIR[:, 512:], WO[l, 1])).astype(BF)
@@ -689,6 +690,11 @@
         both(t1b, l, 2)
         both(t2, l, 0)
 
+        @pl.when(i > 0)
+        def _():
+            both(t5, prev, 2)
+
+
         for h in (0, 1):
             for q in (0, 1):
                 lanes = pl.ds(h * 512 + q * 256, 256)
@@ -729,12 +735,10 @@
 
     for d in (1, 2, 3):
         sc_copy(d).start()
-    both(t5, 1, 0)
-    both(t5, 1, 2)
     both(t4, 0, 0)
     both(t3, 0, 2)
     both(t2, 0, 4)
-    both(t5, 1, 4)
+    both(t5b, 1, 0)
     arrived(RC, sm_r.at[0])
     feature = SGF[:, :, chunk(col, COLS)]
     for d in (0, 1, 2):
@@ -749,8 +753,8 @@
         sd_copy(0, d, z).start()
     both(t3, 0, 4)
     both(t4, 0, 2)
+    both(t5, 1, 4)
     both(t5, 0, 0)
-    both(t5b, 1, 0)
     both(t5b, 1, 2)
     arrived(SZ.at[pl.ds(0, 3)], sm_r.at[1])
     SY[y] = SZ[0] + SZ[1] + SZ[2] + SZ[3]

time: 225 us -> 222 us (0.987)
    pallas_call x1, Pallas kernels: 209 us -> 207 us  [step_call(): pl.pallas_call(kernel, out_shape=[jax.ShapeDtypeStruct((TOK, COLS), BF),...]
where the time goes in v6:
time: 222 us
  Pallas kernels  213 us (96%)
  local copies, waits for them, and re-layouts  8.19 us (4%)
    pallas_call x1, Pallas kernels, step_call(): pl.pallas_call(kernel, out_shape=[jax.ShapeDtypeStruct((TOK, COLS), BF),...  207 us
    unnamed x14, local copies, waits for them, and re-layouts  8.19 us
    pallas_call x1, Pallas kernels, finish_call(): pl.pallas_call(finish_kernel, out_shape=[jax.ShapeDtypeStruct((TOK, COLS)...  6.18 us

profile of v6, /device:TPU:0, one launch (start us, length us, event | category | flops | bytes accessed | tf_op | source)
XLA Modules:
  0.0 221.6 jit_solution(12324463401902006874)
XLA Ops:
  0.6 206.6 %encoder_step.1 = (bf16[256,256]{1,0:T(8,128)(2,1)}, bf16[256,256]{1,0:T(8,128)(2,1)}, bf16[2,3,512,256]{3,2,1,0:T(8,128)(2,1)}, bf16[2,256,512]{2,1,0:T(8,128)(...) custom-call(bf16[256,256]{1,0:T(8,128)(2,1)} %hid.1, ...), custom_call_target="tpu_custom_call" | custom-call | tf_op jit(solution)/shard_map/encoder_step/pallas_call | solution.py:827
  207.2 0.0 copy-start
  207.2 1.6 copy-done
  208.8 0.0 copy-start.1
  208.8 1.6 copy-done.1
  210.4 0.0 copy-start.2
  210.4 1.4 copy-done.2
  211.8 0.0 copy-start.3
  211.8 1.0 copy-done.3
  212.9 0.0 copy-start.4
  212.9 0.9 copy-done.4
  213.8 0.0 copy-start.5
  213.8 0.9 copy-done.5
  214.7 0.0 copy-start.6
  214.7 0.8 copy-done.6
  215.4 6.2 %finish.1 = (bf16[256,256]{1,0:T(8,128)(2,1)}, bf16[256,256]{1,0:T(8,128)(2,1)}, f32[2,2,256]{2,1,0:T(2,128)}, f32[2,256]{1,0:T(2,128)}, f32[2,2,256]{2,1,0:T(2,...) custom-call(bf16[256,256]{1,0:T(8,128)(2,1)S(1)} %copy-done.4, ...), custom_call_target="tpu_custom_call" | custom-call | tf_op jit(solution)/shard_map/finish/pallas_call | solution.py:891
Async XLA Ops:
  207.2 1.6 copy-start
  208.8 1.6 copy-start.1
  210.4 1.4 copy-start.2
  211.8 1.0 copy-start.3
  212.9 0.9 copy-start.4
  213.8 0.9 copy-start.5
  214.7 0.8 copy-start.6
